TPU v7x, 128 devices: a whole 4x4x4 slice. The times are simulated.
128 devices in a mesh: grp: 8 (over y, core), sub: 16 (over z, x).
Axes of the slice: x: 4, y: 4, z: 4, core: 2. Of those that a mesh axis runs over, the one named last changes fastest.
Arguments:
- charges: bfloat16 [32, 1048576], P(None, ('grp', 'sub')), may hold values from -6 to 6
- column_basis: bfloat16 [4096, 64, 256], P(('grp', 'sub')), may hold values from -0.375 to 0.375
- row_basis: bfloat16 [4096, 64, 256], P(('grp', 'sub')), may hold values from -0.75 to 0.75
- local_up: bfloat16 [8064, 64, 64], P(('grp', 'sub')), may hold values from -0.5 to 0.5
- local_down: bfloat16 [8064, 64, 64], P(('grp', 'sub')), may hold values from -0.75 to 0.75
- local_far: int32 [8064, 8], P(('grp', 'sub')), may hold values from 0 to 4095, as said below
- local_coupling: bfloat16 [8064, 8, 64, 64], P(('grp', 'sub')), may hold values from -0.25 to 0.25
- upper_up: bfloat16 [112, 64, 64], P('grp'), may hold values from -0.5 to 0.5
- upper_down: bfloat16 [112, 64, 64], P('grp'), may hold values from -0.75 to 0.75
- upper_far: int32 [120, 8], P('grp'), may hold values from 0 to 63, as said below
- upper_coupling: bfloat16 [120, 8, 64, 64], P('grp'), may hold values from -0.25 to 0.25
- near_source: int32 [4096, 3], P(('grp', 'sub')), may hold values from 0 to 4095, as said below
- near_block: bfloat16 [4096, 3, 256, 256], P(('grp', 'sub')), may hold values from -0.21875 to 0.21875
Outputs:
- potential: bfloat16 [32, 1048576], P(None, ('grp', 'sub'))
Inputs may be any that keep to these rules, and one draw needn't show every extreme that they name: `near_source`: the first near partner of every leaf is the leaf itself; every near partner of a leaf of device d (leaf i lies on d = i div 32) is a leaf of device d-1, d or d+1. `local_far`: each partner is a cluster of the same level, numbered across that level as in the tree step, of device d-1, d or d+1 when the cluster lies on device d. `upper_far`: each partner is a cluster of the same level, numbered across all groups as in the tree step.
All inputs are finite; a program needn't handle non-finite values.
Results may differ from a plain program's by a relative error of at most 0.025.
Values may be sent and summed in bfloat16 or wider, within the bound.
A program may use at most 128 MiB of HBM per device.

v0:
```python
import jax
import jax.numpy as jnp
from jax import lax
from jax.sharding import PartitionSpec as P


def padded(shard, sides, width):
    for axis, dim in sides:
        count, length = (lax.axis_size(axis), shard.shape[dim])
        up = [(i, (i + 1) % count) for i in range(count - 1)]
        down = [(j, i) for i, j in up]
        last = lax.slice_in_dim(shard, length - width, length, axis=dim)
        first = lax.slice_in_dim(shard, 0, width, axis=dim)
        before = lax.ppermute(last, axis, up)
        after = lax.ppermute(first, axis, down)
        shard = jnp.concatenate([before, shard, after], axis=dim)
    return shard


def lift_pairs(transfer, children):
    terms = jnp.einsum("jab,jar->jbr", transfer, children, preferred_element_type=jnp.float32)
    paired = terms.reshape((terms.shape[0] // 2, 2) + terms.shape[1:])
    return (paired[:, 0] + paired[:, 1]).astype(jnp.bfloat16)


def couple(coupling, partners, source):
    picked = jnp.take(source, partners, axis=0)
    return jnp.einsum("tfab,tfbr->tar", coupling, picked, preferred_element_type=jnp.float32)


def descend(transfer, parents, far_terms):
    product = jnp.einsum("jab,jbr->jar", transfer, parents, preferred_element_type=jnp.float32)
    return (far_terms + product).astype(jnp.bfloat16)


def grow_upper(roots, root_up, upper_up):
    batch = roots.shape[0]
    members = roots.shape[1]
    rank = roots.shape[2]
    rhs_width = roots.shape[3]
    current = lift_pairs(
        root_up.reshape((batch * members, rank, rank)),
        roots.reshape((batch * members, rank, rhs_width)),
    )
    current = current.reshape((batch, members // 2, rank, rhs_width))
    grown = [current]
    for height in range(2, members.bit_length()):
        amount = members // 2**height
        offset = members - 4 * amount
        transfer = upper_up[:, offset : offset + 2 * amount].reshape(
            (batch * 2 * amount, rank, rank)
        )
        current = lift_pairs(transfer, current.reshape((batch * 2 * amount, rank, rhs_width)))
        current = current.reshape((batch, amount, rank, rhs_width))
        grown.append(current)
    return jnp.concatenate(grown, axis=1)


def on_device(
    charges,
    column_basis,
    row_basis,
    local_up,
    local_down,
    local_far,
    local_coupling,
    upper_up,
    upper_down,
    upper_far,
    upper_coupling,
    near_source,
    near_block,
):
    leaf_count = column_basis.shape[0]
    rank = column_basis.shape[1]
    leaf_size = column_basis.shape[2]
    rhs_width = charges.shape[0]
    groups = lax.axis_size("grp")
    members = lax.axis_size("sub")
    levels = leaf_count.bit_length() - 1
    device = lax.axis_index("grp") * members + lax.axis_index("sub")
    leaves = charges.reshape((rhs_width, leaf_count, leaf_size))
    moments = [
        jnp.einsum("ika,ria->ikr", column_basis, leaves, preferred_element_type=jnp.float32).astype(
            jnp.bfloat16
        )
    ]
    for height in range(1, levels + 1):
        amount = leaf_count // 2**height
        offset = 2 * leaf_count - 4 * amount
        moments.append(lift_pairs(local_up[offset : offset + 2 * amount], moments[-1]))
    stacked = jnp.concatenate(moments, axis=0)
    local_rows = stacked.shape[0]
    window = padded(charges, ((("grp", "sub"), 1),), leaf_count * leaf_size)
    beside_all = window.reshape((rhs_width, 3 * leaf_count, leaf_size))
    beside = padded(stacked, ((("grp", "sub"), 0),), local_rows)
    beside = beside.reshape((3, local_rows, rank, rhs_width))
    gathered = jnp.take(beside_all, near_source - (device - 1) * leaf_count, axis=1)
    near_terms = jnp.einsum(
        "inab,rinb->ria", near_block, gathered, preferred_element_type=jnp.float32
    )
    far_local = []
    for height in range(levels + 1):
        amount = leaf_count // 2**height
        offset = 2 * leaf_count - 2 * amount
        source = beside[:, offset : offset + amount].reshape((3 * amount, rank, rhs_width))
        partners = local_far[offset : offset + amount] - (device - 1) * amount
        far_local.append(couple(local_coupling[offset : offset + amount], partners, source))
    roots, root_up = (
        lax.all_gather(stacked[-1:], "sub", axis=0, tiled=True),
        lax.all_gather(local_up[-1:], "sub", axis=0, tiled=True),
    )
    mine = grow_upper(roots[None], root_up[None], upper_up[None])[0]
    everyone = lax.all_gather(mine, "grp", axis=0, tiled=True)
    blocks = everyone.reshape((groups, members - 1, rank, rhs_width))
    far_upper = []
    for height in range(1, members.bit_length()):
        amount = members // 2**height
        offset = members - 2 * amount
        source = blocks[:, offset : offset + amount].reshape((groups * amount, rank, rhs_width))
        far_upper.append(
            couple(
                upper_coupling[offset : offset + amount],
                upper_far[offset : offset + amount],
                source,
            )
        )
    current = far_upper[-1].astype(jnp.bfloat16)
    for height in range(members.bit_length() - 2, 0, -1):
        amount = members // 2**height
        offset = members - 2 * amount
        current = descend(
            upper_down[offset : offset + amount],
            jnp.repeat(current, 2, axis=0),
            far_upper[height - 1],
        )
    parent = lax.dynamic_slice_in_dim(current, lax.axis_index("sub") // 2, 1, 0)
    current = descend(local_down[-1:], parent, far_local[levels])
    for height in range(levels - 1, -1, -1):
        amount = leaf_count // 2**height
        offset = 2 * leaf_count - 2 * amount
        current = descend(
            local_down[offset : offset + amount], jnp.repeat(current, 2, axis=0), far_local[height]
        )
    far_out = jnp.einsum("ika,ikr->ria", row_basis, current, preferred_element_type=jnp.float32)
    return (near_terms + far_out).astype(jnp.bfloat16).reshape((rhs_width, leaf_count * leaf_size))


def solution(mesh):
    in_specs = (
        P(None, ("grp", "sub")),
        P(("grp", "sub"), None, None),
        P(("grp", "sub"), None, None),
        P(("grp", "sub"), None, None),
        P(("grp", "sub"), None, None),
        P(("grp", "sub"), None),
        P(("grp", "sub"), None, None, None),
        P("grp", None, None),
        P("grp", None, None),
        P("grp", None),
        P("grp", None, None, None),
        P(("grp", "sub"), None),
        P(("grp", "sub"), None, None, None),
    )
    out_specs = P(None, ("grp", "sub"))
    return jax.shard_map(
        on_device, mesh=mesh, in_specs=in_specs, out_specs=out_specs, check_vma=False
    )
```

profile of v0, /device:TPU:1, one launch (start us, length us, event | category | flops | bytes accessed | tf_op | source)
XLA Modules:
  0.0 159.9 jit_solution(7089460454089633742)
XLA Ops:
  0.0 2.6 %constant_dynamic-update-slice_fusion.5 = (bf16[63,64,32]{1,2,0:T(8,128)(2,1)}, bf16[32,64,32]{1,2,0:T(8,128)(2,1)S(1)}) fusion(bf16[32,64,256]{2,1,0:T(8,128)(2,1)} %param.14, bf16[4,32,8,256]{3,2,1,0:T(8,128)(2,1)} %bitcast.350), kind=kOutput, calls=%fused_computation.171 | convolution fusion | flops 33619968 | bytes 1966080 | tf_op jit(solution)/shard_map/ika,ria->ikr/dot_general | solution.py:84
  6.7 3.9 %collective-permute-start.2 = (bf16[63,64,32]{1,2,0:T(8,128)(2,1)}, bf16[63,64,32]{1,2,0:T(8,128)(2,1)}, u32[]{:S(2)}, u32[]{:S(2)}) collective-permute-start(bf16[63,64,32]{1,2,0:T(8,128)(2,1)} %get-tuple-element.15), channel_id=1, source_target_pairs={{0,1},{1,2},{2,3},{3,4},{4,5},{5,6},{6,7},{7,8},{8,9},{9,10},{10,1... | collective-permute-start | bytes 774152 | tf_op jit(solution)/shard_map/ppermute | solution.py:14
  10.7 7.2 %collective-permute-start.3 = (bf16[63,64,32]{1,2,0:T(8,128)(2,1)}, bf16[63,64,32]{1,2,0:T(8,128)(2,1)}, u32[]{:S(2)}, u32[]{:S(2)}) collective-permute-start(bf16[63,64,32]{1,2,0:T(8,128)(2,1)} %get-tuple-element.15), channel_id=1, source_target_pairs={{1,0},{2,1},{3,2},{4,3},{5,4},{6,5},{7,6},{8,7},{9,8},{10,9},{11,1... | collective-permute-start | bytes 774152 | tf_op jit(solution)/shard_map/ppermute | solution.py:15
  17.9 1.9 %collective-permute-start = (bf16[32,8192]{1,0:T(8,128)(2,1)S(1)}, bf16[32,8192]{1,0:T(8,128)(2,1)}, u32[]{:S(2)}, u32[]{:S(2)}) collective-permute-start(bf16[32,8192]{1,0:T(8,128)(2,1)S(1)} %copy-done.3), channel_id=1, source_target_pairs={{0,1},{1,2},{2,3},{3,4},{4,5},{5,6},{6,7},{7,8},{8,9},{9,10},{10,1... | collective-permute-start | bytes 1572872 | tf_op jit(solution)/shard_map/ppermute | solution.py:14
  19.8 7.0 %collective-permute-start.1 = (bf16[32,8192]{1,0:T(8,128)(2,1)S(1)}, bf16[32,8192]{1,0:T(8,128)(2,1)}, u32[]{:S(2)}, u32[]{:S(2)}) collective-permute-start(bf16[32,8192]{1,0:T(8,128)(2,1)S(1)} %copy-done.3), channel_id=1, source_target_pairs={{1,0},{2,1},{3,2},{4,3},{5,4},{6,5},{7,6},{8,7},{9,8},{10,9},{11,1... | collective-permute-start | bytes 1572872 | tf_op jit(solution)/shard_map/ppermute | solution.py:15
  26.8 24.8 %all-gather = bf16[16,1,64,32]{2,3,1,0:T(8,128)(2,1)S(1)} all-gather(bf16[1,1,64,32]{2,3,1,0:T(8,128)(2,1)S(1)} %get-tuple-element.16), channel_id=2, replica_groups=mesh['grp'=8,'sub'=16] {'sub'}, dimensions={0}, use_global_device_ids=true | all-gather | bytes 69632 | tf_op jit(solution)/shard_map/all_gather | solution.py:110
  51.6 17.7 %all_gather.10 = bf16[16,64,64]{2,1,0:T(8,128)(2,1)S(1)} all-gather(bf16[1,64,64]{2,1,0:T(8,128)(2,1)S(1)} %slice-done), channel_id=1, replica_groups=mesh['grp'=8,'sub'=16] {'sub'}, dimensions={0}, use_global_device_ids=true | all-gather | bytes 139264 | tf_op jit(solution)/shard_map/all_gather | solution.py:111
  70.3 26.1 %all-gather.1 = bf16[1,120,64,32]{2,3,0,1:T(8,128)(2,1)S(1)} all-gather(bf16[1,15,64,32]{2,3,0,1:T(8,128)(2,1)S(1)} %pad_maximum_fusion.1), channel_id=3, replica_groups=mesh['grp'=8,'sub'=16] {'grp'}, dimensions={1}, use_global_device_ids=true | all-gather | bytes 552960 | tf_op jit(solution)/shard_map/all_gather | solution.py:114
  108.8 1.2 convolution_bitcast_fusion.6
  110.0 1.1 fusion.39
  111.8 1.4 convolution_bitcast_fusion.2
  114.8 2.4 %convolution_bitcast_fusion = f32[8,32,64]{2,1,0:T(8,128)} fusion(bf16[15,8,64,64]{3,2,1,0:T(8,128)(2,1)} %param.23, bf16[8,8,64,32]{2,3,1,0:T(8,128)(2,1)S(1)} %bitcast.348, pred[8,8]{1,0:T(8,128)(4,1)} %copy.132), kind=kOutput, calls=%fused_computation.36 | convolution fusion | flops 16908288 | bytes 1377280 | tf_op jit(solution)/shard_map/tfab,tfbr->tar/dot_general | solution.py:28
  122.8 1.1 convolution_bitcast_fusion.9
  123.9 1.2 convolution_bitcast_fusion.7
  127.5 1.4 convolution_bitcast_fusion.3
  130.5 1.7 %convolution_bitcast_fusion.1 = f32[8,32,64]{2,1,0:T(8,128)S(1)} fusion(bf16[63,8,64,64]{3,2,1,0:T(8,128)(2,1)} %param.19, bf16[8,8,64,32]{2,3,1,0:T(8,128)(2,1)S(1)} %bitcast.349, pred[8,8]{1,0:T(8,128)(4,1)S(1)} %copy.126), kind=kOutput, calls=%fused_computation.37 | convolution fusion | flops 16908288 | bytes 1376320 | tf_op jit(solution)/shard_map/tfab,tfbr->tar/dot_general | solution.py:28
  134.1 2.4 %fusion.21 = f32[16,32,64]{2,1,0:T(8,128)S(1)} fusion(bf16[63,8,64,64]{3,2,1,0:T(8,128)(2,1)} %param.19, bf16[16,8,64,32]{2,3,1,0:T(8,128)(2,1)S(1)} %bitcast.334, pred[16,8]{1,0:T(8,128)(4,1)S(1)} %copy.124), kind=kOutput, calls=%fused_computation.32 | convolution fusion | flops 33816576 | bytes 2752640 | tf_op jit(solution)/shard_map/tfab,tfbr->tar/dot_general | solution.py:28
  136.5 1.2 fusion.25
  137.8 2.2 %gather_fusion.1 = bf16[256,64,32]{1,2,0:T(8,128)(2,1)} fusion(bf16[96,64,32]{1,2,0:T(8,128)(2,1)S(1)} %bitcast.326, s32[1024]{0:T(1024)S(1)} %get-tuple-element.37), kind=kCustom, calls=%fused_computation.1 | custom fusion | bytes 2098176 | tf_op jit(solution)/shard_map/jit(_take)/gather | solution.py:27
  140.0 4.9 %fusion.14 = f32[32,32,64]{2,1,0:T(8,128)} fusion(bf16[63,8,64,64]{3,2,1,0:T(8,128)(2,1)} %param.19, bf16[32,8,64,32]{2,3,1,0:T(8,128)(2,1)} %bitcast.330, pred[32,8]{1,0:T(8,128)(4,1)S(1)} %copy.113), kind=kOutput, calls=%fused_computation.26 | convolution fusion | flops 67633152 | bytes 6553856 | tf_op jit(solution)/shard_map/tfab,tfbr->tar/dot_general | solution.py:28
  144.9 1.3 pad_maximum_fusion
  146.5 2.0 %gather_fusion = bf16[96,32,256]{2,1,0:T(8,128)(2,1)} fusion(bf16[32,96,256]{2,0,1:T(8,128)(2,1)S(1)} %bitcast.328, s32[1024]{0:T(1024)S(1)} %get-tuple-element.38), kind=kCustom, calls=%fused_computation | custom fusion | bytes 3146112 | tf_op jit(solution)/shard_map/jit(_take)/gather | solution.py:98
  148.4 8.8 %fusion.10 = f32[32,32,256]{2,1,0:T(8,128)S(1)} fusion(bf16[32,3,256,256]{3,2,1,0:T(8,128)(2,1)} %param.25, bf16[32,3,32,256]{3,2,1,0:T(8,128)(2,1)} %bitcast.329, pred[32,3]{1,0:T(8,128)(4,1)S(1)} %copy.110), kind=kOutput, calls=%fused_computation.23 | convolution fusion | flops 403439616 | bytes 15204448 | tf_op jit(solution)/shard_map/inab,rinb->ria/dot_general | solution.py:99
  157.3 1.8 %fusion.19 = bf16[32,4,8,256]{3,2,1,0:T(8,128)(2,1)S(1)} fusion(f32[32,32,256]{2,1,0:T(8,128)S(1)} %fusion.10, bf16[32,64,256]{2,1,0:T(8,128)(2,1)S(1)} %copy-done, f32[32,32,64]{2,1,0:T(8,128)} %fusion.14, bf16[32,64,32]{1,2,0:T(8,128)(2,1)S(1)} %bitcast.358, bf16[63,64,64]{2,1,0:T(8,128)(2,1)} %param.17), kind=kOutput, calls=%fused_computation.27 | convolution fusion | flops 42598400 | bytes 3801088 | tf_op jit(solution)/shard_map/ika,ikr->ria/dot_general | solution.py:145
  (156 shorter events, 32.0 us)
Async XLA Ops:
  0.0 157.3 %copy-start = (bf16[32,64,256]{2,1,0:T(8,128)(2,1)S(1)}, bf16[32,64,256]{2,1,0:T(8,128)(2,1)}, u32[]{:S(2)}) copy-start(bf16[32,64,256]{2,1,0:T(8,128)(2,1)} %param.15) | copy-start | bytes 3145732
  0.0 2.6 %copy-start.4 = (bf16[63,64,64]{2,1,0:T(8,128)(2,1)S(1)}, bf16[63,64,64]{2,1,0:T(8,128)(2,1)}, u32[]{:S(2)}) copy-start(bf16[63,64,64]{2,1,0:T(8,128)(2,1)} %param.16) | copy-start | bytes 1548292
  2.6 15.3 %copy-start.3 = (bf16[32,8192]{1,0:T(8,128)(2,1)S(1)}, bf16[32,8192]{1,0:T(8,128)(2,1)}, u32[]{:S(2)}) copy-start(bf16[32,8192]{1,0:T(8,128)(2,1)} %param.13) | copy-start | bytes 1572868
  2.6 48.9 %slice-start = ((bf16[63,64,64]{2,1,0:T(8,128)(2,1)}), bf16[1,64,64]{2,1,0:T(8,128)(2,1)S(1)}, s32[]{:S(2)}) async-start(bf16[63,64,64]{2,1,0:T(8,128)(2,1)} %param.16), calls=%async_computation | async-start | bytes 32768 | tf_op jit(solution)/shard_map/slice | solution.py:111
  2.9 66.6 %copy-start.6 = (bf16[14,64,64]{2,1,0:T(8,128)(2,1)S(1)}, bf16[14,64,64]{2,1,0:T(8,128)(2,1)}, u32[]{:S(2)}) copy-start(bf16[14,64,64]{2,1,0:T(8,128)(2,1)} %param.20) | copy-start | bytes 344068
  3.8 66.2 %copy-start.5 = (s32[15,8]{0,1:T(8,128)S(1)}, s32[15,8]{0,1:T(8,128)}, u32[]{:S(2)}) copy-start(s32[15,8]{0,1:T(8,128)} %param.22) | copy-start | bytes 1444
  6.7 111.3 %collective-permute-start.2 = (bf16[63,64,32]{1,2,0:T(8,128)(2,1)}, bf16[63,64,32]{1,2,0:T(8,128)(2,1)}, u32[]{:S(2)}, u32[]{:S(2)}) collective-permute-start(bf16[63,64,32]{1,2,0:T(8,128)(2,1)} %get-tuple-element.15), channel_id=1, source_target_pairs={{0,1},{1,2},{2,3},{3,4},{4,5},{5,6},{6,7},{7,8},{8,9},{9,10},{10,1... | collective-permute-start | bytes 774152 | tf_op jit(solution)/shard_map/ppermute | solution.py:14
  10.7 108.6 %collective-permute-start.3 = (bf16[63,64,32]{1,2,0:T(8,128)(2,1)}, bf16[63,64,32]{1,2,0:T(8,128)(2,1)}, u32[]{:S(2)}, u32[]{:S(2)}) collective-permute-start(bf16[63,64,32]{1,2,0:T(8,128)(2,1)} %get-tuple-element.15), channel_id=1, source_target_pairs={{1,0},{2,1},{3,2},{4,3},{5,4},{6,5},{7,6},{8,7},{9,8},{10,9},{11,1... | collective-permute-start | bytes 774152 | tf_op jit(solution)/shard_map/ppermute | solution.py:15
  17.9 127.0 %collective-permute-start = (bf16[32,8192]{1,0:T(8,128)(2,1)S(1)}, bf16[32,8192]{1,0:T(8,128)(2,1)}, u32[]{:S(2)}, u32[]{:S(2)}) collective-permute-start(bf16[32,8192]{1,0:T(8,128)(2,1)S(1)} %copy-done.3), channel_id=1, source_target_pairs={{0,1},{1,2},{2,3},{3,4},{4,5},{5,6},{6,7},{7,8},{8,9},{9,10},{10,1... | collective-permute-start | bytes 1572872 | tf_op jit(solution)/shard_map/ppermute | solution.py:14
  19.8 125.1 %collective-permute-start.1 = (bf16[32,8192]{1,0:T(8,128)(2,1)S(1)}, bf16[32,8192]{1,0:T(8,128)(2,1)}, u32[]{:S(2)}, u32[]{:S(2)}) collective-permute-start(bf16[32,8192]{1,0:T(8,128)(2,1)S(1)} %copy-done.3), channel_id=1, source_target_pairs={{1,0},{2,1},{3,2},{4,3},{5,4},{6,5},{7,6},{8,7},{9,8},{10,9},{11,1... | collective-permute-start | bytes 1572872 | tf_op jit(solution)/shard_map/ppermute | solution.py:15
  69.9 27.5 %copy-start.8 = (s32[63,8]{0,1:T(8,128)S(1)}, s32[63,8]{0,1:T(8,128)}, u32[]{:S(2)}) copy-start(s32[63,8]{0,1:T(8,128)} %param.18) | copy-start | bytes 6052
  69.9 36.4 %copy-start.15 = (s32[32,3]{0,1:T(4,128)S(1)}, s32[32,3]{0,1:T(4,128)}, u32[]{:S(2)}) copy-start(s32[32,3]{0,1:T(4,128)} %param.24) | copy-start | bytes 1156
  99.0 14.2 %copy-start.7 = (bf16[14,64,64]{2,1,0:T(8,128)(2,1)S(1)}, bf16[14,64,64]{2,1,0:T(8,128)(2,1)}, u32[]{:S(2)}) copy-start(bf16[14,64,64]{2,1,0:T(8,128)(2,1)} %param.21) | copy-start | bytes 344068
  108.3 5.2 %copy-start.10 = (s32[8]{0:T(128)S(1)}, s32[8]{0:T(128)}, u32[]{:S(2)}) copy-start(s32[8]{0:T(128)} %fusion.136) | copy-start | bytes 100
  114.1 3.1 %copy-start.11 = (s32[32]{0:T(128)S(1)}, s32[32]{0:T(128)}, u32[]{:S(2)}) copy-start(s32[32]{0:T(128)} %reshape.387) | copy-start | bytes 388
  114.1 3.1 %copy-start.19 = (s32[16]{0:T(128)S(1)}, s32[16]{0:T(128)}, u32[]{:S(2)}) copy-start(s32[16]{0:T(128)} %reshape.395) | copy-start | bytes 196
  114.1 3.1 %copy-start.12 = (s32[128]{0:T(128)S(1)}, s32[128]{0:T(128)}, u32[]{:S(2)}) copy-start(s32[128]{0:T(128)} %reshape.371) | copy-start | bytes 1540
  114.1 3.1 %copy-start.13 = (s32[64]{0:T(128)S(1)}, s32[64]{0:T(128)}, u32[]{:S(2)}) copy-start(s32[64]{0:T(128)} %reshape.379) | copy-start | bytes 772
  114.1 3.1 %copy-start.14 = (s32[96]{0:T(128)S(1)}, s32[96]{0:T(128)}, u32[]{:S(2)}) copy-start(s32[96]{0:T(128)} %reshape.355) | copy-start | bytes 1156
  114.1 3.1 %copy-start.17 = (pred[2,8]{0,1:T(8,128)(4,1)S(1)}, pred[2,8]{0,1:T(8,128)(4,1)}, u32[]{:S(2)}) copy-start(pred[2,8]{0,1:T(8,128)(4,1)} %get-tuple-element.5) | copy-start | bytes 52
  114.2 3.2 %copy-start.16 = (pred[4,8]{0,1:T(8,128)(4,1)S(1)}, pred[4,8]{0,1:T(8,128)(4,1)}, u32[]{:S(2)}) copy-start(pred[4,8]{0,1:T(8,128)(4,1)} %get-tuple-element.7) | copy-start | bytes 100
  114.2 3.6 %copy-start.9 = (pred[32,3]{0,1:T(4,128)(4,1)S(1)}, pred[32,3]{0,1:T(4,128)(4,1)}, u32[]{:S(2)}) copy-start(pred[32,3]{0,1:T(4,128)(4,1)} %get-tuple-element.25) | copy-start | bytes 292
  119.2 3.6 %copy-start.18 = (pred[8]{0:T(512)(128)(4,1)S(1)}, pred[8]{0:T(512)(128)(4,1)}, u32[]{:S(2)}) copy-start(pred[8]{0:T(512)(128)(4,1)} %and_reduce_fusion.1) | copy-start | bytes 28
  134.1 3.7 %copy-start.2 = (bf16[189,64,32]{1,2,0:T(8,128)(2,1)S(1)}, bf16[189,64,32]{1,2,0:T(8,128)(2,1)}, u32[]{:S(2)}) copy-start(bf16[189,64,32]{1,2,0:T(8,128)(2,1)} %copy-done.1) | copy-start | bytes 2322436
  (1 other events, 1.2 us)
where the time goes:
time: 161 us; the launch traced here: 160 us
  blocking collectives  68.6 us (43%)
  matrix products  38.8 us (24%)
  local copies, waits for them, and re-layouts  21.7 us (13%)
  starting transfers between devices  20 us (12%)
  other arithmetic  10 us (6%)
    all_gather x1, blocking collectives, on_device(): everyone = lax.all_gather(mine, 'grp', axis=0, tiled=True)  26.1 us
    all_gather x1, blocking collectives, on_device(): lax.all_gather(stacked[-1:], 'sub', axis=0, tiled=True)  24.8 us
    dot_general x10, matrix products, couple(): jnp.einsum('tfab,tfbr->tar', coupling, picked, preferred_element_type=jnp...  18.7 us
    all_gather x1, blocking collectives, on_device(): lax.all_gather(local_up[-1:], 'sub', axis=0, tiled=True)  17.7 us
    ppermute x2, starting transfers between devices, padded(): after = lax.ppermute(first, axis, down)  14.2 us
    dot_general x1, matrix products, on_device(): jnp.einsum('inab,rinb->ria', near_block, gathered, preferred_element_type...  8.82 us
    gather x10, local copies, waits for them, and re-layouts, couple(): picked = jnp.take(source, partners, axis=0)  7.79 us
    ppermute x2, starting transfers between devices, padded(): before = lax.ppermute(last, axis, up)  5.86 us
  transfers between devices with their start and end apart: 4, of which 0 were waited for; matrix products, arithmetic and copies ran while one was open for 30% of the time, Pallas kernels for 0%

commit v1 on v0

v1 whole, which is shorter than its diff:
```python
import jax
import jax.numpy as jnp
from jax import lax
from jax.experimental import pallas as pl
from jax.experimental.pallas import tpu as pltpu
from jax.sharding import PartitionSpec as P

MESH = pl.DeviceIdType.MESH
BF = jnp.bfloat16
F32 = jnp.float32
RHS = 32
LEAVES = 32
LEAF = 256
RANK = 64
LEVELS = 5
COLS = LEAVES * LEAF
MROW = 64 * RANK
XCHUNKS = 16
XW = COLS // XCHUNKS
DEPTH = 3


def nt(a, b):
    return lax.dot_general(a, b, (((1,), (1,)), ((), ())), preferred_element_type=F32)


def nn(a, b):
    return lax.dot_general(a, b, (((1,), (0,)), ((), ())), preferred_element_type=F32)


def lanes(start, size):
    return pl.ds(pl.multiple_of(start, 128), size)


def loop(count, body, unroll):
    def step(i, carry):
        body(i)
        return carry

    lax.fori_loop(0, count, step, 0, unroll=min(unroll, count))


def row_of(height):
    return 64 - 2 * (LEAVES >> height)


def kernel(
    charges,
    column_basis,
    row_basis,
    local_up,
    local_down,
    local_far,
    local_coupling,
    upper_up,
    upper_down,
    upper_far,
    upper_coupling,
    near_source,
    near_block,
    out,
    cx,
    xin,
    xw,
    cbv,
    rbv,
    upv,
    dnv,
    cpv,
    uuv,
    udv,
    ucv,
    nbv,
    mw,
    lo,
    hi,
    rx,
    rz,
    rg,
    acc,
    far,
    dloc,
    gall,
    ov,
    far_at,
    ufar_at,
    near_at,
    lsem,
    osem,
    xsend,
    xrecv,
    msend,
    mrecv,
    rxsend,
    rxrecv,
    rzsend,
    rzrecv,
    rgsend,
    rgrecv,
):
    g = lax.axis_index("grp")
    s = lax.axis_index("sub")
    d = g * 16 + s
    z = s // 4
    x = s % 4

    def place(e):
        return (e // 16, e % 16)

    right = place((d + 1) % 128)
    left = place((d + 127) % 128)
    by_x = [(g, z * 4 + (x + k) % 4) for k in range(1, 4)]
    by_z = [(g, ((z + k) % 4) * 4 + x) for k in range(1, 4)]
    by_g = [((g + k) % 8, s) for k in range(1, 8)]
    peers = [right, left] + by_x + by_z + by_g

    barrier = pltpu.get_barrier_semaphore()
    for peer in peers:
        pl.semaphore_signal(barrier, inc=1, device_id=peer, device_id_type=MESH)

    loads = []

    def load(src, dst):
        copy = pltpu.make_async_copy(src, dst, lsem.at[len(loads)])
        copy.start()
        loads.append(copy)
        return copy

    get_x = load(charges, cx)
    get_cb = [load(column_basis.at[pl.ds(8 * k, 8)], cbv.at[pl.ds(8 * k, 8)]) for k in range(4)]
    get_up = load(local_up, upv)
    get_at = [load(local_far, far_at), load(upper_far, ufar_at), load(near_source, near_at)]
    get_uu = load(upper_up, uuv)

    pl.semaphore_wait(barrier, len(peers))

    def send(src, dst, ssem, rsem, peer):
        copy = pltpu.make_async_remote_copy(
            src_ref=src, dst_ref=dst, send_sem=ssem, recv_sem=rsem, device_id=peer, device_id_type=MESH
        )
        copy.start()
        return copy

    sent = []

    def advance(count):
        for _ in range(count):
            k = len(sent)
            if k >= XCHUNKS:
                return
            if k >= DEPTH:
                for copy in sent[k - DEPTH]:
                    copy.wait_send()
            src = charges.at[:, pl.ds(k * XW, XW)]
            sent.append(
                [
                    send(src, xin.at[0, :, pl.ds(k * XW, XW)], xsend.at[0, k], xrecv.at[0, k], right),
                    send(src, xin.at[1, :, pl.ds(k * XW, XW)], xsend.at[1, k], xrecv.at[1, k], left),
                ]
            )

    advance(DEPTH)

    get_nb = [load(near_block.at[pl.ds(4 * k, 4)], nbv.at[pl.ds(4 * k, 4)]) for k in range(8)]
    get_dn = load(local_down, dnv)
    get_cp = [load(local_coupling.at[pl.ds(9 * k, 9)], cpv.at[pl.ds(9 * k, 9)]) for k in range(7)]
    get_ud = [
        load(upper_down.at[16 - (32 >> k) + s // 2**k], udv.at[k - 1]) for k in range(1, 4)
    ]
    get_uc = [
        load(upper_coupling.at[16 - (32 >> k) + s // 2**k], ucv.at[k - 1]) for k in range(1, 5)
    ]
    get_rb = load(row_basis, rbv)

    low = lax.broadcasted_iota(jnp.int32, (RHS, 128), 1) < 64

    get_x.wait()
    for k in range(4):
        get_cb[k].wait()

        def leaf_moments(i):
            at = 4 * k + i
            one, two = cx[:, lanes(512 * at, 256)], cx[:, lanes(512 * at + 256, 256)]
            xw[LEAVES + 2 * at] = one
            xw[LEAVES + 2 * at + 1] = two
            pair = jnp.concatenate([one, two], axis=0)
            both = nt(pair, cbv[pl.ds(2 * at, 2)].reshape(128, LEAF))
            mw[:, lanes(MROW + 128 * at, 128)] = jnp.where(low, both[:RHS], both[RHS:]).astype(BF)

        loop(4, leaf_moments, 4)

    def send_moments(k, start, size):
        src = mw.at[:, pl.ds(MROW + start, size)]
        return [
            send(src, mw.at[:, pl.ds(start, size)], msend.at[0, k], mrecv.at[0, k], right),
            send(src, mw.at[:, pl.ds(2 * MROW + start, size)], msend.at[1, k], mrecv.at[1, k], left),
        ]

    moved = [send_moments(0, 0, 2048)]

    get_up.wait()
    zero = jnp.zeros((RHS, RANK), F32)
    for height in range(1, LEVELS + 1):
        amount = LEAVES >> height
        base, child = row_of(height), row_of(height - 1)

        def lift(j):
            pair = mw[:, lanes(MROW + child * 64 + 128 * j, 128)]
            return nn(pair, upv[pl.ds(child + 2 * j, 2)].reshape(128, RANK))

        if amount == 1:
            root = lift(0)
            mw[:, pl.ds(MROW + base * 64, 128)] = jnp.concatenate([root, zero], axis=1).astype(BF)
        else:

            def lift_two(j):
                both = jnp.concatenate([lift(2 * j), lift(2 * j + 1)], axis=1)
                mw[:, lanes(MROW + base * 64 + 128 * j, 128)] = both.astype(BF)

            loop(amount // 2, lift_two, 4)
    moved.append(send_moments(1, 2048, 2048))

    lifted = nn(root.astype(BF), upv[62])
    rx[x] = jnp.where(low == (x < 2), jnp.concatenate([lifted, lifted], axis=1), 0.0).astype(BF)
    gone_x = [send(rx.at[x], rx.at[x], rxsend.at[k], rxrecv.at[k], p) for k, p in enumerate(by_x)]

    advance(1)
    get_at[2].wait()

    def near_own(i):
        acc[:, lanes(256 * i, 256)] = nt(xw[LEAVES + i], nbv[i, 0])

    for k in range(4):
        get_nb[k].wait()
        loop(4, lambda i: near_own(4 * k + i), 4)
        if k == 1:
            advance(1)

    get_uu.wait()
    for copy in gone_x:
        copy.wait_recv()
    first = (
        (rx[0].astype(F32) + rx[1].astype(F32)) + (rx[2].astype(F32) + rx[3].astype(F32))
    ).astype(BF)
    second = nn(first, uuv[pl.ds(2 * z, 2)].reshape(128, RANK))
    rz[z, :, 0:128] = first
    rz[z, :, 128:256] = jnp.where(
        low == (z % 2 == 0), jnp.concatenate([second, second], axis=1), 0.0
    ).astype(BF)
    gone_z = [send(rz.at[z], rz.at[z], rzsend.at[k], rzrecv.at[k], p) for k, p in enumerate(by_z)]

    advance(1)
    for k in range(4, 8):
        get_nb[k].wait()
        loop(4, lambda i: near_own(4 * k + i), 4)
        if k == 5:
            advance(1)

    for copy in gone_z:
        copy.wait_recv()
    for k in range(4):
        rg[g, k] = rz[k, :, 0:128]
    thirds = []
    for k in range(2):
        pair = (
            rz[2 * k, :, 128:256].astype(F32) + rz[2 * k + 1, :, 128:256].astype(F32)
        ).astype(BF)
        rg[g, 4 + k] = pair
        thirds.append(nn(pair, uuv[8 + 2 * k : 10 + 2 * k].reshape(128, RANK)))
    third = jnp.concatenate(thirds, axis=1).astype(BF)
    rg[g, 6] = third
    top = nn(third, uuv[12:14].reshape(128, RANK))
    rg[g, 7] = jnp.concatenate([top, zero], axis=1).astype(BF)
    gone_g = [send(rg.at[g], rg.at[g], rgsend.at[k], rgrecv.at[k], p) for k, p in enumerate(by_g)]

    advance(1)

    get_dn.wait()
    gall[pl.ds(62 * 64, 64)] = dnv[62]
    for height in range(LEVELS - 1, -1, -1):
        amount = LEAVES >> height
        base, parent = row_of(height), row_of(height + 1)

        def extend(j):
            pair = dnv[pl.ds(base + 2 * j, 2)].reshape(128, RANK)
            above = gall[pl.ds(pl.multiple_of((parent + j) * 64, 64), 64)]
            gall[pl.ds(pl.multiple_of((base + 2 * j) * 64, 128), 128)] = nn(pair, above).astype(BF)

        loop(amount // 2, extend, 4)
    for copy in get_ud:
        copy.wait()
    down1 = udv[0]
    down2 = nn(down1, udv[1]).astype(BF)
    down3 = nn(down2, udv[2]).astype(BF)
    advance(1)

    get_at[0].wait()
    for copy in get_cp:
        copy.wait()
    for pair_of in moved:
        for copy in pair_of:
            copy.wait_recv()
    blank = jnp.zeros((RHS, RANK), BF)

    def spread(i):
        pair = mw[:, lanes(128 * i, 128)]
        even, odd = pair[:, :64], pair[:, 64:]
        lo[2 * i] = jnp.concatenate([even, blank], axis=1)
        hi[2 * i] = jnp.concatenate([blank, even], axis=1)
        lo[2 * i + 1] = jnp.concatenate([odd, blank], axis=1)
        hi[2 * i + 1] = jnp.concatenate([blank, odd], axis=1)

    loop(96, spread, 4)
    advance(1)

    for height in range(LEVELS, -1, -1):
        amount = LEAVES >> height
        base = row_of(height)
        bits = LEVELS - height

        def couple(t):
            def at(f):
                q = far_at[f, t] - (d - 1) * amount
                return ((q >> bits) & 3) * 64 + base + (q & (amount - 1))

            total = None
            for q in range(2):
                moments = jnp.concatenate(
                    [lo[at(4 * q + 2 * j)] + hi[at(4 * q + 2 * j + 1)] for j in range(2)], axis=1
                )
                blocks = jnp.concatenate([cpv[t, 4 * q + j] for j in range(4)], axis=1)
                term = nt(moments, blocks)
                total = term if total is None else total + term
            return total

        if amount == 1:
            far[:, pl.ds(base * 64, 128)] = jnp.concatenate([couple(base), zero], axis=1)
        else:

            def couple_two(j):
                t = base + 2 * j
                far[:, lanes(base * 64 + 128 * j, 128)] = jnp.concatenate(
                    [couple(t), couple(t + 1)], axis=1
                )

            if amount == 32:
                for k in range(4):
                    loop(4, lambda j: couple_two(4 * k + j), 4)
                    advance(1)
            else:
                loop(amount // 2, couple_two, 4)
                if amount == 8 or amount == 16:
                    advance(1)

    dloc[:, pl.ds(62 * 64, 128)] = far[:, pl.ds(62 * 64, 128)].astype(BF)
    for height in range(LEVELS - 1, -1, -1):
        amount = LEAVES >> height
        base, parent = row_of(height), row_of(height + 1)

        def descend(at, above):
            pair = dnv[pl.ds(base + 2 * at, 2)].reshape(128, RANK)
            here = lanes(base * 64 + 128 * at, 128)
            total = far[:, here] + nt(above, pair)
            if height == 0:
                far[:, here] = total
            else:
                dloc[:, here] = total.astype(BF)

        if amount == 2:
            descend(0, dloc[:, pl.ds(62 * 64, 128)][:, :64])
        else:

            def descend_two(j):
                above = dloc[:, lanes(parent * 64 + 128 * j, 128)]
                descend(2 * j, above[:, :64])
                descend(2 * j + 1, above[:, 64:])

            loop(amount // 4, descend_two, 4)
    advance(XCHUNKS)

    get_at[1].wait()
    for copy in get_uc:
        copy.wait()
    for copy in gone_g:
        copy.wait_recv()
    terms = []
    for k in range(1, 5):
        amount = 16 >> k
        base = 16 - 2 * amount
        row = base + s // 2**k

        def pick(f):
            p = ufar_at[f, row]
            r = base + (p & (amount - 1))
            pair = rg[p >> (4 - k), r >> 1].astype(F32)
            turned = jnp.concatenate([pair[:, 64:], pair[:, :64]], axis=1)
            keep = (1 - (r + f) % 2).astype(F32)
            return pair * keep + turned * (1.0 - keep)

        total = None
        for q in range(2):
            moments = jnp.concatenate(
                [jnp.where(low, pick(4 * q + 2 * j), pick(4 * q + 2 * j + 1)) for j in range(2)], axis=1
            ).astype(BF)
            blocks = jnp.concatenate([ucv[k - 1, 4 * q + j] for j in range(4)], axis=1)
            term = nt(moments, blocks)
            total = term if total is None else total + term
        terms.append(total)
    parent = (
        terms[0]
        + nt(terms[1].astype(BF), down1)
        + nt(terms[2].astype(BF), down2)
        + nt(terms[3].astype(BF), down3)
    ).astype(BF)

    get_rb.wait()

    def expand(i):
        wide = lanes(128 * i, 128)
        path = gall[pl.ds(pl.multiple_of(128 * i, 128), 128)]
        both = far[:, wide] + nt(parent, path)
        split = jnp.concatenate(
            [jnp.where(low, both, 0.0), jnp.where(low, 0.0, both)], axis=0
        ).astype(BF)
        res = nn(split, rbv[pl.ds(2 * i, 2)].reshape(128, LEAF))
        acc[:, lanes(512 * i, 256)] += res[:RHS]
        acc[:, lanes(512 * i + 256, 256)] += res[RHS:]

    loop(16, expand, 4)

    for k, pair_of in enumerate(sent):
        for copy in pair_of:
            copy.wait_recv()
        for side in range(2):
            for i in range(XW // LEAF):
                at = k * (XW // LEAF) + i
                xw[2 * LEAVES * side + at] = xin[side, :, 256 * at : 256 * (at + 1)]

    put = []
    for k in range(4):

        def near_rest(j):
            i = 8 * k + j
            here = lanes(256 * i, 256)
            total = acc[:, here]
            for n in (1, 2):
                q = (near_at[n, i] - (d - 1) * LEAVES) & 127
                total = total + nt(xw[q], nbv[i, n])
            ov[:, here] = total.astype(BF)

        loop(8, near_rest, 8)
        part = pl.ds(2048 * k, 2048)
        copy = pltpu.make_async_copy(ov.at[:, part], out.at[:, part], osem.at[k])
        copy.start()
        put.append(copy)

    for copy in put:
        copy.wait()
    for pair_of in sent[XCHUNKS - DEPTH :]:
        for copy in pair_of:
            copy.wait_send()
    for pair_of in moved:
        for copy in pair_of:
            copy.wait_send()
    for copy in gone_x + gone_z + gone_g:
        copy.wait_send()


def on_device(
    charges,
    column_basis,
    row_basis,
    local_up,
    local_down,
    local_far,
    local_coupling,
    upper_up,
    upper_down,
    upper_far,
    upper_coupling,
    near_source,
    near_block,
):
    dma = pltpu.SemaphoreType.DMA
    vmem = pltpu.VMEM
    anywhere = pl.BlockSpec(memory_space=pl.ANY)
    return pl.pallas_call(
        kernel,
        out_shape=jax.ShapeDtypeStruct((RHS, COLS), BF),
        in_specs=[anywhere] * 13,
        out_specs=anywhere,
        scratch_shapes=[
            vmem((RHS, COLS), BF),
            vmem((2, RHS, COLS), BF),
            vmem((4 * LEAVES, RHS, LEAF), BF),
            vmem((LEAVES, RANK, LEAF), BF),
            vmem((LEAVES, RANK, LEAF), BF),
            vmem((63, RANK, RANK), BF),
            vmem((63, RANK, RANK), BF),
            vmem((63, 8, RANK, RANK), BF),
            vmem((14, RANK, RANK), BF),
            vmem((3, RANK, RANK), BF),
            vmem((4, 8, RANK, RANK), BF),
            vmem((LEAVES, 3, LEAF, LEAF), BF),
            vmem((RHS, 3 * MROW), BF),
            vmem((256, RHS, 128), BF),
            vmem((256, RHS, 128), BF),
            vmem((4, RHS, 128), BF),
            vmem((4, RHS, 256), BF),
            vmem((8, 8, RHS, 128), BF),
            vmem((RHS, COLS), F32),
            vmem((RHS, MROW), F32),
            vmem((RHS, MROW), BF),
            vmem((MROW, RANK), BF),
            vmem((RHS, COLS), BF),
            pltpu.SMEM((8, 63), jnp.int32),
            pltpu.SMEM((8, 15), jnp.int32),
            pltpu.SMEM((3, LEAVES), jnp.int32),
            dma((40,)),
            dma((4,)),
            dma((2, XCHUNKS)),
            dma((2, XCHUNKS)),
            dma((2, 2)),
            dma((2, 2)),
            dma((3,)),
            dma((3,)),
            dma((3,)),
            dma((3,)),
            dma((7,)),
            dma((7,)),
        ],
        compiler_params=pltpu.CompilerParams(
            collective_id=0, has_side_effects=True, vmem_limit_bytes=60 * 2**20
        ),
        name="h2_product",
    )(
        charges,
        column_basis,
        row_basis,
        local_up,
        local_down,
        local_far.T,
        local_coupling,
        upper_up,
        upper_down,
        upper_far.T,
        upper_coupling,
        near_source.T,
        near_block,
    )


def solution(mesh):
    both = ("grp", "sub")
    in_specs = (
        P(None, both),
        P(both, None, None),
        P(both, None, None),
        P(both, None, None),
        P(both, None, None),
        P(both, None),
        P(both, None, None, None),
        P("grp", None, None),
        P("grp", None, None),
        P("grp", None),
        P("grp", None, None, None),
        P(both, None),
        P(both, None, None, None),
    )
    return jax.shard_map(
        on_device, mesh=mesh, in_specs=in_specs, out_specs=P(None, both), check_vma=False
    )
```

time: 161 us -> 46.2 us (0.29)
  the two profiles are of different devices: /device:TPU:1 before, /device:TPU:0 now
where the time goes in v1:
time: 46.2 us; the launch traced here: 46 us
  Pallas kernels  44.2 us (96%)
  local copies, waits for them, and re-layouts  1.87 us (4%)
    pallas_call x1, Pallas kernels, on_device(): pl.pallas_call(kernel, out_shape=jax.ShapeDtypeStruct((RHS, COLS), BF), i...  44.2 us
    unnamed x1, local copies, waits for them, and re-layouts  1.87 us

profile of v1, /device:TPU:0, one launch (start us, length us, event | category | flops | bytes accessed | tf_op | source)
XLA Modules:
  0.0 46.0 jit_solution(639283736903038608)
XLA Ops:
  0.0 44.2 %h2_product.1 = bf16[32,8192]{1,0:T(8,128)(2,1)} custom-call(bf16[32,8192]{1,0:T(8,128)(2,1)} %charges.1, bf16[32,64,256]{2,1,0:T(8,128)(2,1)} %column_basis.1, bf16[32,64,256]{2,1,0:T(8,128)(2,1)} %row_basis.1, bf16[63,64,64]{2,1,0:T(8,128)(2,1)} %local_up.1, bf16[63,64,64]{2,1,0:T(8,128)(2,1)} %local_down.1, s32[8,63]{1,0:T(8,128)} %bitcast.3, ...), custom_call_target="tpu_custom_call" | custom-call | tf_op jit(solution)/shard_map/h2_product/pallas_call | solution.py:487
  44.2 1.9 %copy.15 = bf16[32,8192]{1,0:T(8,128)(2,1)} copy(bf16[32,8192]{1,0:T(8,128)(2,1)} %h2_product.1) | data formatting | bytes 1048576

commit v2 on v1

v2 whole, which is shorter than its diff:
```python
import jax
import jax.numpy as jnp
from jax import lax
from jax.experimental import pallas as pl
from jax.experimental.pallas import tpu as pltpu
from jax.sharding import PartitionSpec as P

MESH = pl.DeviceIdType.MESH
BF = jnp.bfloat16
F32 = jnp.float32
RHS = 32
LEAVES = 32
LEAF = 256
RANK = 64
LEVELS = 5
COLS = LEAVES * LEAF
XPARTS = ((0, 1024), (1024, 1024), (2048, 2048), (4096, 2048), (6144, 2048))
XFIRST = 2
OWN, REACH, TURN, FAR, REST, FINISH = 4, 16, 96, 16, 8, 16


def nt(a, b):
    return lax.dot_general(a, b, (((1,), (1,)), ((), ())), preferred_element_type=F32)


def nn(a, b):
    return lax.dot_general(a, b, (((1,), (0,)), ((), ())), preferred_element_type=F32)


def lanes(start, size):
    return pl.ds(pl.multiple_of(start, 128), size)


def loop(count, body, unroll):
    def step(i, carry):
        body(i)
        return carry

    lax.fori_loop(0, count, step, 0, unroll=min(unroll, count))


def batched(count, width, compute, store):
    width = min(width, count)

    def body(b):
        got = [compute(width * b + j) for j in range(width)]
        for j in range(width):
            store(width * b + j, got[j])

    loop(count // width, body, 1)


def row_of(height):
    return 64 - 2 * (LEAVES >> height)


def kernel(
    charges,
    column_basis,
    row_basis,
    local_up,
    local_down,
    local_far,
    local_coupling,
    upper_up,
    upper_down,
    upper_far,
    upper_coupling,
    near_source,
    near_block,
    out,
    cx,
    xin,
    xw,
    cbv,
    rbv,
    upv,
    dnv,
    cpv,
    uuv,
    udv,
    ucv,
    nbv,
    mv,
    rx,
    rz,
    rg,
    acc,
    far,
    dloc,
    path,
    qv,
    far_raw,
    far_row,
    far_at,
    ufar_at,
    near_at,
    lsem,
    xsend,
    xrecv,
    msend,
    mrecv,
    rxsend,
    rxrecv,
    rzsend,
    rzrecv,
    rgsend,
    rgrecv,
):
    g = lax.axis_index("grp")
    s = lax.axis_index("sub")
    d = g * 16 + s
    z = s // 4
    x = s % 4

    def place(e):
        return (e // 16, e % 16)

    sides = ((d < 127, place((d + 1) % 128)), (d > 0, place((d + 127) % 128)))
    by_x = [(g, z * 4 + (x + k) % 4) for k in range(1, 4)]
    by_z = [(g, ((z + k) % 4) * 4 + x) for k in range(1, 4)]
    by_g = [((g + k) % 8, s) for k in range(1, 8)]
    peers = by_x + by_z + by_g

    barrier = pltpu.get_barrier_semaphore()
    for peer in peers:
        pl.semaphore_signal(barrier, inc=1, device_id=peer, device_id_type=MESH)
    for there, peer in sides:

        @pl.when(there)
        def _():
            pl.semaphore_signal(barrier, inc=1, device_id=peer, device_id_type=MESH)

    loads = []

    def load(src, dst):
        copy = pltpu.make_async_copy(src, dst, lsem.at[len(loads)])
        copy.start()
        loads.append(copy)
        return copy

    get_x = [load(charges.at[:, pl.ds(4096 * k, 4096)], cx.at[:, pl.ds(4096 * k, 4096)]) for k in range(2)]
    get_cb = [load(column_basis.at[pl.ds(8 * k, 8)], cbv.at[pl.ds(8 * k, 8)]) for k in range(4)]
    get_up = load(local_up, upv)
    get_uu = load(upper_up, uuv)
    get_at = [load(local_far, far_raw), load(upper_far, ufar_at), load(near_source, near_at)]

    pl.semaphore_wait(barrier, len(peers) + (d < 127).astype(jnp.int32) + (d > 0).astype(jnp.int32))

    def remote(src, dst, ssem, rsem, peer):
        return pltpu.make_async_remote_copy(
            src_ref=src, dst_ref=dst, send_sem=ssem, recv_sem=rsem, device_id=peer, device_id_type=MESH
        )

    def send(src, dst, ssem, rsem, peer):
        copy = remote(src, dst, ssem, rsem, peer)
        copy.start()
        return copy

    def beside(src, dst, ssem, rsem):
        return [remote(src, dst(2 * k), ssem.at[k], rsem.at[k], peer) for k, (_, peer) in enumerate(sides)]

    def start(batches, straight=True, turning=True):
        for k, (there, _) in enumerate(sides):
            turns = x == 3 - 3 * k
            go = there
            if not turning:
                go = there & jnp.logical_not(turns)
            elif not straight:
                go = there & turns

            @pl.when(go)
            def _():
                for copies in batches:
                    copies[k].start()

    def arrive(copies):
        for (there, _), copy in zip((sides[1], sides[0]), copies):
            pl.when(there)(copy.wait_recv)

    def leave(copies):
        for (there, _), copy in zip(sides, copies):
            pl.when(there)(copy.wait_send)

    def charges_part(k):
        start, size = XPARTS[k]
        part = pl.ds(start, size)
        return beside(
            charges.at[:, part],
            lambda side: xin.at[side // 2, :, part],
            xsend.at[k],
            xrecv.at[k],
        )

    sent = [charges_part(k) for k in range(len(XPARTS))]
    start(sent[:XFIRST])

    get_ud = [
        load(upper_down.at[16 - (32 >> k) + s // 2**k], udv.at[k - 1]) for k in range(1, 4)
    ]
    get_uc = [
        load(upper_coupling.at[16 - (32 >> k) + s // 2**k], ucv.at[k - 1]) for k in range(1, 5)
    ]

    low = lax.broadcasted_iota(jnp.int32, (RHS, 128), 1) < 64

    for k in range(4):
        if k % 2 == 0:
            get_x[k // 2].wait()
        get_cb[k].wait()

        def leaf_moments(i):
            at = 4 * k + i
            one, two = cx[:, lanes(512 * at, 256)], cx[:, lanes(512 * at + 256, 256)]
            both = nt(jnp.concatenate([one, two], axis=0), cbv[pl.ds(2 * at, 2)].reshape(128, LEAF))
            return one, two, jnp.where(low, both[:RHS], both[RHS:]).astype(BF)

        def keep_moments(i, got):
            at = 4 * k + i
            xw[LEAVES + 2 * at] = got[0]
            xw[LEAVES + 2 * at + 1] = got[1]
            mv[32 + at] = got[2]

        batched(4, 4, leaf_moments, keep_moments)

    get_up.wait()
    zero = jnp.zeros((RHS, RANK), F32)
    for height in range(1, LEVELS + 1):
        amount = LEAVES >> height
        base, child = row_of(height), row_of(height - 1)

        def lift(j):
            return nn(mv[32 + child // 2 + j], upv[pl.ds(child + 2 * j, 2)].reshape(128, RANK))

        def lift_two(j):
            return jnp.concatenate([lift(2 * j), lift(2 * j + 1)], axis=1).astype(BF)

        def keep_two(j, got):
            mv[32 + base // 2 + j] = got

        if amount == 1:
            root = lift(0)
            mv[63] = jnp.concatenate([root, zero], axis=1).astype(BF)
        else:
            batched(amount // 2, 4, lift_two, keep_two)

    get_dn = load(local_down, dnv)
    get_nb = [load(near_block.at[pl.ds(4 * k, 4)], nbv.at[pl.ds(4 * k, 4)]) for k in range(8)]
    get_cp = [load(local_coupling.at[pl.ds(9 * k, 9)], cpv.at[pl.ds(9 * k, 9)]) for k in range(7)]
    get_rb = load(row_basis, rbv)

    lifted = nn(root.astype(BF), upv[62])
    rx[x] = jnp.where(low == (x < 2), jnp.concatenate([lifted, lifted], axis=1), 0.0).astype(BF)
    gone_x = [send(rx.at[x], rx.at[x], rxsend.at[k], rxrecv.at[k], p) for k, p in enumerate(by_x)]
    moved = [
        beside(
            mv.at[pl.ds(32 + 16 * k, 16)],
            lambda side: mv.at[pl.ds(32 * side + 16 * k, 16)],
            msend.at[k],
            mrecv.at[k],
        )
        for k in range(2)
    ]
    start(moved + sent[XFIRST:], turning=False)
    start(moved[:1], straight=False)

    get_at[0].wait()
    t = lax.broadcasted_iota(jnp.int32, (8, 63), 1)
    f = lax.broadcasted_iota(jnp.int32, (8, 63), 0)
    amount = jnp.full((8, 63), LEAVES, jnp.int32)
    for height in range(1, LEVELS + 1):
        amount = jnp.where(t < row_of(height), amount, LEAVES >> height)
    q = far_raw[...] - (d - 1) * amount
    window = (q >= amount).astype(jnp.int32) + (q >= 2 * amount).astype(jnp.int32)
    row = 64 - 2 * amount + (q & (amount - 1))
    far_row[...] = jnp.zeros((8, 64), jnp.int32)
    far_row[:, 0:63] = ((row + f) & 1) * 128 + window * 32 + (row >> 1)
    get_far = pltpu.make_async_copy(far_row, far_at, lsem.at[len(loads)])
    get_far.start()

    get_dn.wait()

    def extend_level(height):
        amount = LEAVES >> height
        base, parent = row_of(height), row_of(height + 1)

        def below(above, j):
            return nt(above, dnv[pl.ds(base + 2 * j, 2)].reshape(128, RANK)).astype(BF)

        if amount == 2:
            path[base // 2] = below(dnv[62].T, 0)
        else:

            def extend(j):
                above = path[parent // 2 + j]
                return below(above[:, :64], 2 * j), below(above[:, 64:], 2 * j + 1)

            def keep(j, got):
                path[base // 2 + 2 * j] = got[0]
                path[base // 2 + 2 * j + 1] = got[1]

            batched(amount // 4, 4, extend, keep)

    for height in range(LEVELS - 1, -1, -1):
        extend_level(height)

    get_uu.wait()
    for copy in gone_x:
        copy.wait_recv()
    first = (
        (rx[0].astype(F32) + rx[1].astype(F32)) + (rx[2].astype(F32) + rx[3].astype(F32))
    ).astype(BF)
    rz[z, 0] = first
    second = nn(first, uuv[pl.ds(2 * z, 2)].reshape(128, RANK))
    rz[z, 1] = jnp.where(low == (z % 2 == 0), jnp.concatenate([second, second], axis=1), 0.0).astype(BF)
    gone_z = [send(rz.at[z], rz.at[z], rzsend.at[k], rzrecv.at[k], p) for k, p in enumerate(by_z)]
    start(moved[1:], straight=False)

    def near_own(i):
        return nt(xw[LEAVES + i], nbv[i, 0])

    def keep_own(i, got):
        acc[:, lanes(256 * i, 256)] = got

    for k in range(4):
        get_nb[k].wait()
        batched(4, OWN, lambda i: near_own(4 * k + i), lambda i, got: keep_own(4 * k + i, got))

    for copy in gone_z:
        copy.wait_recv()
    for k in range(4):
        rg[g, k] = rz[k, 0]
    thirds = []
    for k in range(2):
        pair = (rz[2 * k, 1].astype(F32) + rz[2 * k + 1, 1].astype(F32)).astype(BF)
        rg[g, 4 + k] = pair
        thirds.append(nn(pair, uuv[8 + 2 * k : 10 + 2 * k].reshape(128, RANK)))
    third = jnp.concatenate(thirds, axis=1).astype(BF)
    rg[g, 6] = third
    top = nn(third, uuv[12:14].reshape(128, RANK))
    rg[g, 7] = jnp.concatenate([top, zero], axis=1).astype(BF)
    gone_g = [send(rg.at[g], rg.at[g], rgsend.at[k], rgrecv.at[k], p) for k, p in enumerate(by_g)]
    start(sent[XFIRST:], straight=False)

    for k in range(4, 8):
        get_nb[k].wait()
        batched(4, OWN, lambda i: near_own(4 * k + i), lambda i, got: keep_own(4 * k + i, got))

    get_rb.wait()

    def reach(i):
        pair = path[i]
        return nn(pair[:, :64], rbv[2 * i]).astype(BF), nn(pair[:, 64:], rbv[2 * i + 1]).astype(BF)

    def keep_reach(i, got):
        qv[:, lanes(512 * i, 256)] = got[0]
        qv[:, lanes(512 * i + 256, 256)] = got[1]

    batched(16, REACH, reach, keep_reach)
    for copy in get_ud:
        copy.wait()
    down1 = udv[0]
    down2 = nn(down1, udv[1]).astype(BF)
    down3 = nn(down2, udv[2]).astype(BF)

    for copies in moved:
        arrive(copies)

    def turn(i):
        pair = mv[i]
        return jnp.concatenate([pair[:, 64:], pair[:, :64]], axis=1)

    def keep_turn(i, got):
        mv[128 + i] = got

    batched(96, TURN, turn, keep_turn)
    get_far.wait()
    for copy in get_cp:
        copy.wait()

    def couple(t):
        total = None
        for q in range(2):
            moments = jnp.concatenate(
                [
                    jnp.where(low, mv[far_at[4 * q + 2 * j, t]], mv[far_at[4 * q + 2 * j + 1, t]])
                    for j in range(2)
                ],
                axis=1,
            )
            blocks = jnp.concatenate([cpv[t, 4 * q + j] for j in range(4)], axis=1)
            term = nt(moments, blocks)
            total = term if total is None else total + term
        return total

    def couple_two(j):
        return jnp.concatenate([couple(2 * j), couple(2 * j + 1)], axis=1)

    def keep_couple(j, got):
        far[j] = got

    batched(32, FAR, couple_two, keep_couple)

    dloc[31] = far[31].astype(BF)
    for height in range(LEVELS - 1, -1, -1):
        amount = LEAVES >> height
        base, parent = row_of(height), row_of(height + 1)

        def below(above, j):
            pair = dnv[pl.ds(base + 2 * j, 2)].reshape(128, RANK)
            return (far[base // 2 + j] + nt(above, pair)).astype(BF)

        if amount == 2:
            dloc[base // 2] = below(dloc[31][:, :64], 0)
        else:

            def descend(j):
                above = dloc[parent // 2 + j]
                return below(above[:, :64], 2 * j), below(above[:, 64:], 2 * j + 1)

            def keep_descend(j, got):
                dloc[base // 2 + 2 * j] = got[0]
                dloc[base // 2 + 2 * j + 1] = got[1]

            batched(amount // 4, 4, descend, keep_descend)

    def local(i):
        pair = dloc[i]
        return [
            acc[:, lanes(512 * i + 256 * k, 256)] + nn(pair[:, 64 * k : 64 * (k + 1)], rbv[2 * i + k])
            for k in range(2)
        ]

    def keep_rest(i, got):
        for k in range(2):
            acc[:, lanes(512 * i + 256 * k, 256)] = got[k]

    batched(16, 8, local, keep_rest)

    get_at[2].wait()
    for copies, (start, size) in zip(sent, XPARTS):
        arrive(copies)

        def window(i):
            part = lanes(start + LEAF * i, LEAF)
            return xin[0, :, part], xin[1, :, part]

        def keep_window(i, got):
            xw[start // LEAF + i] = got[0]
            xw[2 * LEAVES + start // LEAF + i] = got[1]

        batched(size // LEAF, 4, window, keep_window)

    def rest(i):
        totals = []
        for k in range(2):
            leaf = 2 * i + k
            total = acc[:, lanes(256 * leaf, 256)]
            for n in (1, 2):
                q = (near_at[n, leaf] - (d - 1) * LEAVES) & 127
                total = total + nt(xw[q], nbv[leaf, n])
            totals.append(total)
        return totals

    batched(16, REST, rest, keep_rest)

    get_at[1].wait()
    for copy in get_uc:
        copy.wait()
    for copy in gone_g:
        copy.wait_recv()
    terms = []
    for k in range(1, 5):
        amount = 16 >> k
        row = 16 - 2 * amount + s // 2**k

        def pick(f):
            p = ufar_at[f, row]
            group, j = p >> (4 - k), p & (amount - 1)
            pair = rg[group, (0, 4, 6, 7)[k - 1] + (j >> 1)]
            pair = pair.astype(F32)
            turned = jnp.concatenate([pair[:, 64:], pair[:, :64]], axis=1)
            keep = (1 - ((j + f) & 1)).astype(F32)
            return pair * keep + turned * (1.0 - keep)

        total = None
        for q in range(2):
            moments = jnp.concatenate(
                [jnp.where(low, pick(4 * q + 2 * j), pick(4 * q + 2 * j + 1)) for j in range(2)], axis=1
            ).astype(BF)
            blocks = jnp.concatenate([ucv[k - 1, 4 * q + j] for j in range(4)], axis=1)
            term = nt(moments, blocks)
            total = term if total is None else total + term
        terms.append(total)
    parent = (
        terms[0]
        + nt(terms[1].astype(BF), down1)
        + nt(terms[2].astype(BF), down2)
        + nt(terms[3].astype(BF), down3)
    ).astype(BF)

    def finish(i):
        part = lanes(512 * i, 512)
        return (acc[:, part] + nn(parent, qv[:, part])).astype(BF)

    def keep_finish(i, got):
        out[:, lanes(512 * i, 512)] = got

    batched(16, FINISH, finish, keep_finish)

    for copies in sent:
        leave(copies)
    for copies in moved:
        leave(copies)
    for copy in gone_x + gone_z + gone_g:
        copy.wait_send()


def on_device(
    charges,
    column_basis,
    row_basis,
    local_up,
    local_down,
    local_far,
    local_coupling,
    upper_up,
    upper_down,
    upper_far,
    upper_coupling,
    near_source,
    near_block,
):
    dma = pltpu.SemaphoreType.DMA
    vmem = pltpu.VMEM
    anywhere = pl.BlockSpec(memory_space=pl.ANY)
    return pl.pallas_call(
        kernel,
        out_shape=pltpu.VMEM((RHS, COLS), BF),
        in_specs=[anywhere] * 13,
        out_specs=pl.BlockSpec(memory_space=vmem),
        scratch_shapes=[
            vmem((RHS, COLS), BF),
            vmem((2, RHS, COLS), BF),
            vmem((4 * LEAVES, RHS, LEAF), BF),
            vmem((LEAVES, RANK, LEAF), BF),
            vmem((LEAVES, RANK, LEAF), BF),
            vmem((63, RANK, RANK), BF),
            vmem((63, RANK, RANK), BF),
            vmem((64, 8, RANK, RANK), BF),
            vmem((14, RANK, RANK), BF),
            vmem((3, RANK, RANK), BF),
            vmem((4, 8, RANK, RANK), BF),
            vmem((LEAVES, 3, LEAF, LEAF), BF),
            vmem((256, RHS, 128), BF),
            vmem((4, RHS, 128), BF),
            vmem((4, 2, RHS, 128), BF),
            vmem((8, 8, RHS, 128), BF),
            vmem((RHS, COLS), F32),
            vmem((32, RHS, 128), F32),
            vmem((32, RHS, 128), BF),
            vmem((32, RANK, 128), BF),
            vmem((RANK, COLS), BF),
            vmem((8, 63), jnp.int32),
            vmem((8, 64), jnp.int32),
            pltpu.SMEM((8, 64), jnp.int32),
            pltpu.SMEM((8, 15), jnp.int32),
            pltpu.SMEM((3, LEAVES), jnp.int32),
            dma((40,)),
            dma((len(XPARTS), 2)),
            dma((len(XPARTS), 2)),
            dma((2, 2)),
            dma((2, 2)),
            dma((3,)),
            dma((3,)),
            dma((3,)),
            dma((3,)),
            dma((7,)),
            dma((7,)),
        ],
        compiler_params=pltpu.CompilerParams(
            collective_id=0, has_side_effects=True, vmem_limit_bytes=60 * 2**20
        ),
        name="h2_product",
    )(
        charges,
        column_basis,
        row_basis,
        local_up,
        local_down,
        local_far.T,
        local_coupling,
        upper_up,
        upper_down,
        upper_far.T,
        upper_coupling,
        near_source.T,
        near_block,
    )


def solution(mesh):
    both = ("grp", "sub")
    in_specs = (
        P(None, both),
        P(both, None, None),
        P(both, None, None),
        P(both, None, None),
        P(both, None, None),
        P(both, None),
        P(both, None, None, None),
        P("grp", None, None),
        P("grp", None, None),
        P("grp", None),
        P("grp", None, None, None),
        P(both, None),
        P(both, None, None, None),
    )
    return jax.shard_map(
        on_device, mesh=mesh, in_specs=in_specs, out_specs=P(None, both), check_vma=False
    )
```

time: 46.2 us -> 37.7 us (0.82)
  the two profiles are of different devices: /device:TPU:0 before, /device:TPU:1 now
where the time goes in v2:
time: 37.7 us; the launch traced here: 37.5 us
  Pallas kernels  36.7 us (97%)
  local copies, waits for them, and re-layouts  0.8 us (2%)
    pallas_call x1, Pallas kernels, on_device(): pl.pallas_call(kernel, out_shape=pltpu.VMEM((RHS, COLS), BF), in_specs=[a...  36.7 us
    unnamed x1, local copies, waits for them, and re-layouts  0.8 us

profile of v2, /device:TPU:1, one launch (start us, length us, event | category | flops | bytes accessed | tf_op | source)
XLA Modules:
  0.0 37.5 jit_solution(13596152678411134627)
XLA Ops:
  0.0 36.7 %h2_product.1 = bf16[32,8192]{1,0:T(8,128)(2,1)S(1)} custom-call(bf16[32,8192]{1,0:T(8,128)(2,1)} %charges.1, bf16[32,64,256]{2,1,0:T(8,128)(2,1)} %column_basis.1, bf16[32,64,256]{2,1,0:T(8,128)(2,1)} %row_basis.1, bf16[63,64,64]{2,1,0:T(8,128)(2,1)} %local_up.1, bf16[63,64,64]{2,1,0:T(8,128)(2,1)} %local_down.1, s32[8,63]{1,0:T(8,128)} %bitcast.3, ...), custom_call_target="tpu_custom_call" | custom-call | tf_op jit(solution)/shard_map/h2_product/pallas_call | solution.py:537
  36.7 0.8 %copy.15 = bf16[32,8192]{1,0:T(8,128)(2,1)} copy(bf16[32,8192]{1,0:T(8,128)(2,1)S(1)} %h2_product.1) | data formatting | bytes 1048576

commit v3 on v2

--- a/solution.py
+++ b/solution.py
@@ -1,3 +1,5 @@
+import functools
+
 import jax
 import jax.numpy as jnp
 from jax import lax
@@ -85,6 +87,7 @@
     rx,
     rz,
     rg,
+    pv,
     acc,
     far,
     dloc,
@@ -106,6 +109,8 @@
     rzrecv,
     rgsend,
     rgrecv,
+    psend,
+    precv,
 ):
     g = lax.axis_index("grp")
     s = lax.axis_index("sub")
@@ -117,19 +122,33 @@
         return (e // 16, e % 16)
 
     sides = ((d < 127, place((d + 1) % 128)), (d > 0, place((d + 127) % 128)))
-    by_x = [(g, z * 4 + (x + k) % 4) for k in range(1, 4)]
+    inner = (x == 1) | (x == 2)
+    outer = jnp.logical_not(inner)
+    y, core = g // 2, g % 2
+    middle = [(g, z * 4 + 1), (g, z * 4 + 2)]
+    other = (g, z * 4 + 3 - x)
+    helped = (g, z * 4 + 3 * (x // 2))
     by_z = [(g, ((z + k) % 4) * 4 + x) for k in range(1, 4)]
-    by_g = [((g + k) % 8, s) for k in range(1, 8)]
-    peers = by_x + by_z + by_g
+    by_y = [(((y + k) % 4) * 2 + core, s) for k in range(1, 4)]
+    twin = (2 * y + 1 - core, s)
 
     barrier = pltpu.get_barrier_semaphore()
-    for peer in peers:
+
+    def greet(peer):
         pl.semaphore_signal(barrier, inc=1, device_id=peer, device_id_type=MESH)
+
     for there, peer in sides:
-
-        @pl.when(there)
-        def _():
-            pl.semaphore_signal(barrier, inc=1, device_id=peer, device_id_type=MESH)
+        pl.when(there)(functools.partial(greet, peer))
+
+    @pl.when(inner)
+    def _():
+        for peer in [other, (g, z * 4), (g, z * 4 + 3)] + by_z + by_y + [twin]:
+            greet(peer)
+
+    @pl.when(outer)
+    def _():
+        for peer in middle:
+            greet(peer)
 
     loads = []
 
@@ -145,7 +164,9 @@
     get_uu = load(upper_up, uuv)
     get_at = [load(local_far, far_raw), load(upper_far, ufar_at), load(near_source, near_at)]
 
-    pl.semaphore_wait(barrier, len(peers) + (d < 127).astype(jnp.int32) + (d > 0).astype(jnp.int32))
+    @pl.when(outer)
+    def _():
+        pl.semaphore_wait(barrier, 2 + (d < 127).astype(jnp.int32) + (d > 0).astype(jnp.int32))
 
     def remote(src, dst, ssem, rsem, peer):
         return pltpu.make_async_remote_copy(
@@ -160,16 +181,10 @@
     def beside(src, dst, ssem, rsem):
         return [remote(src, dst(2 * k), ssem.at[k], rsem.at[k], peer) for k, (_, peer) in enumerate(sides)]
 
-    def start(batches, straight=True, turning=True):
+    def start(batches):
         for k, (there, _) in enumerate(sides):
-            turns = x == 3 - 3 * k
-            go = there
-            if not turning:
-                go = there & jnp.logical_not(turns)
-            elif not straight:
-                go = there & turns
-
-            @pl.when(go)
+
+            @pl.when(there)
             def _():
                 for copies in batches:
                     copies[k].start()
@@ -193,7 +208,7 @@
         )
 
     sent = [charges_part(k) for k in range(len(XPARTS))]
-    start(sent[:XFIRST])
+    pl.when(outer)(lambda: start(sent[:XFIRST]))
 
     get_ud = [
         load(upper_down.at[16 - (32 >> k) + s // 2**k], udv.at[k - 1]) for k in range(1, 4)
@@ -251,7 +266,24 @@
 
     lifted = nn(root.astype(BF), upv[62])
     rx[x] = jnp.where(low == (x < 2), jnp.concatenate([lifted, lifted], axis=1), 0.0).astype(BF)
-    gone_x = [send(rx.at[x], rx.at[x], rxsend.at[k], rxrecv.at[k], p) for k, p in enumerate(by_x)]
+
+    @pl.when(inner)
+    def _():
+        pl.semaphore_wait(barrier, 12)
+
+    gone_x = [remote(rx.at[x], rx.at[x], rxsend.at[0], rxrecv.at[0], other)] + [
+        remote(rx.at[x], rx.at[x], rxsend.at[1 + k], rxrecv.at[1 + x // 3], p) for k, p in enumerate(middle)
+    ]
+
+    @pl.when(inner)
+    def _():
+        gone_x[0].start()
+
+    @pl.when(outer)
+    def _():
+        gone_x[1].start()
+        gone_x[2].start()
+
     moved = [
         beside(
             mv.at[pl.ds(32 + 16 * k, 16)],
@@ -261,8 +293,9 @@
         )
         for k in range(2)
     ]
-    start(moved + sent[XFIRST:], turning=False)
-    start(moved[:1], straight=False)
+    start(moved)
+    pl.when(inner)(lambda: start(sent[:XFIRST]))
+    start(sent[XFIRST:])
 
     get_at[0].wait()
     t = lax.broadcasted_iota(jnp.int32, (8, 63), 1)
@@ -305,16 +338,20 @@
         extend_level(height)
 
     get_uu.wait()
-    for copy in gone_x:
-        copy.wait_recv()
-    first = (
-        (rx[0].astype(F32) + rx[1].astype(F32)) + (rx[2].astype(F32) + rx[3].astype(F32))
-    ).astype(BF)
-    rz[z, 0] = first
-    second = nn(first, uuv[pl.ds(2 * z, 2)].reshape(128, RANK))
-    rz[z, 1] = jnp.where(low == (z % 2 == 0), jnp.concatenate([second, second], axis=1), 0.0).astype(BF)
-    gone_z = [send(rz.at[z], rz.at[z], rzsend.at[k], rzrecv.at[k], p) for k, p in enumerate(by_z)]
-    start(moved[1:], straight=False)
+    gone_z = [remote(rz.at[z], rz.at[z], rzsend.at[k], rzrecv.at[k], p) for k, p in enumerate(by_z)]
+
+    @pl.when(inner)
+    def _():
+        for k in range(3):
+            remote(rx.at[k], rx.at[k], rxsend.at[k], rxrecv.at[k], other).wait_recv()
+        first = (
+            (rx[0].astype(F32) + rx[1].astype(F32)) + (rx[2].astype(F32) + rx[3].astype(F32))
+        ).astype(BF)
+        rz[z, 0] = first
+        second = nn(first, uuv[pl.ds(2 * z, 2)].reshape(128, RANK))
+        rz[z, 1] = jnp.where(low == (z % 2 == 0), jnp.concatenate([second, second], axis=1), 0.0).astype(BF)
+        for copy in gone_z:
+            copy.start()
 
     def near_own(i):
         return nt(xw[LEAVES + i], nbv[i, 0])
@@ -326,21 +363,25 @@
         get_nb[k].wait()
         batched(4, OWN, lambda i: near_own(4 * k + i), lambda i, got: keep_own(4 * k + i, got))
 
-    for copy in gone_z:
-        copy.wait_recv()
-    for k in range(4):
-        rg[g, k] = rz[k, 0]
-    thirds = []
-    for k in range(2):
-        pair = (rz[2 * k, 1].astype(F32) + rz[2 * k + 1, 1].astype(F32)).astype(BF)
-        rg[g, 4 + k] = pair
-        thirds.append(nn(pair, uuv[8 + 2 * k : 10 + 2 * k].reshape(128, RANK)))
-    third = jnp.concatenate(thirds, axis=1).astype(BF)
-    rg[g, 6] = third
-    top = nn(third, uuv[12:14].reshape(128, RANK))
-    rg[g, 7] = jnp.concatenate([top, zero], axis=1).astype(BF)
-    gone_g = [send(rg.at[g], rg.at[g], rgsend.at[k], rgrecv.at[k], p) for k, p in enumerate(by_g)]
-    start(sent[XFIRST:], straight=False)
+    gone_y = [remote(rg.at[g], rg.at[g], rgsend.at[k], rgrecv.at[k], p) for k, p in enumerate(by_y + [twin])]
+
+    @pl.when(inner)
+    def _():
+        for copy in gone_z:
+            copy.wait_recv()
+        for k in range(4):
+            rg[g, k] = rz[k, 0]
+        thirds = []
+        for k in range(2):
+            pair = (rz[2 * k, 1].astype(F32) + rz[2 * k + 1, 1].astype(F32)).astype(BF)
+            rg[g, 4 + k] = pair
+            thirds.append(nn(pair, uuv[8 + 2 * k : 10 + 2 * k].reshape(128, RANK)))
+        third = jnp.concatenate(thirds, axis=1).astype(BF)
+        rg[g, 6] = third
+        top = nn(third, uuv[12:14].reshape(128, RANK))
+        rg[g, 7] = jnp.concatenate([top, zero], axis=1).astype(BF)
+        for copy in gone_y:
+            copy.start()
 
     for k in range(4, 8):
         get_nb[k].wait()
@@ -467,37 +508,54 @@
     get_at[1].wait()
     for copy in get_uc:
         copy.wait()
-    for copy in gone_g:
-        copy.wait_recv()
-    terms = []
-    for k in range(1, 5):
-        amount = 16 >> k
-        row = 16 - 2 * amount + s // 2**k
-
-        def pick(f):
-            p = ufar_at[f, row]
-            group, j = p >> (4 - k), p & (amount - 1)
-            pair = rg[group, (0, 4, 6, 7)[k - 1] + (j >> 1)]
-            pair = pair.astype(F32)
-            turned = jnp.concatenate([pair[:, 64:], pair[:, :64]], axis=1)
-            keep = (1 - ((j + f) & 1)).astype(F32)
-            return pair * keep + turned * (1.0 - keep)
-
-        total = None
-        for q in range(2):
-            moments = jnp.concatenate(
-                [jnp.where(low, pick(4 * q + 2 * j), pick(4 * q + 2 * j + 1)) for j in range(2)], axis=1
-            ).astype(BF)
-            blocks = jnp.concatenate([ucv[k - 1, 4 * q + j] for j in range(4)], axis=1)
-            term = nt(moments, blocks)
-            total = term if total is None else total + term
-        terms.append(total)
-    parent = (
-        terms[0]
-        + nt(terms[1].astype(BF), down1)
-        + nt(terms[2].astype(BF), down2)
-        + nt(terms[3].astype(BF), down3)
-    ).astype(BF)
+    passed = []
+    for k in range(3):
+        from_y = ((y + 3 - k) % 4) * 2 + core
+        passed.append(remote(rg.at[from_y], rg.at[from_y], rgsend.at[4 + k], rgrecv.at[4 + k], twin))
+    gone_p = remote(pv, pv, psend, precv, helped)
+
+    @pl.when(inner)
+    def _():
+        for k in (0, 2, 1):
+            gone_y[k].wait_recv()
+            passed[k].start()
+        gone_y[3].wait_recv()
+        for copy in passed:
+            copy.wait_recv()
+        terms = []
+        for k in range(1, 5):
+            amount = 16 >> k
+            row = 16 - 2 * amount + s // 2**k
+
+            def pick(f):
+                p = ufar_at[f, row]
+                group, j = p >> (4 - k), p & (amount - 1)
+                pair = rg[group, (0, 4, 6, 7)[k - 1] + (j >> 1)]
+                pair = pair.astype(F32)
+                turned = jnp.concatenate([pair[:, 64:], pair[:, :64]], axis=1)
+                keep = (1 - ((j + f) & 1)).astype(F32)
+                return pair * keep + turned * (1.0 - keep)
+
+            total = None
+            for q in range(2):
+                moments = jnp.concatenate(
+                    [jnp.where(low, pick(4 * q + 2 * j), pick(4 * q + 2 * j + 1)) for j in range(2)], axis=1
+                ).astype(BF)
+                blocks = jnp.concatenate([ucv[k - 1, 4 * q + j] for j in range(4)], axis=1)
+                term = nt(moments, blocks)
+                total = term if total is None else total + term
+            terms.append(total)
+        parent = (
+            terms[0]
+            + nt(terms[1].astype(BF), down1)
+            + nt(terms[2].astype(BF), down2)
+            + nt(terms[3].astype(BF), down3)
+        ).astype(BF)
+        pv[...] = jnp.concatenate([parent, parent], axis=1)
+        gone_p.start()
+
+    pl.when(outer)(gone_p.wait_recv)
+    parent = pv[...][:, :64]
 
     def finish(i):
         part = lanes(512 * i, 512)
@@ -512,8 +570,16 @@
         leave(copies)
     for copies in moved:
         leave(copies)
-    for copy in gone_x + gone_z + gone_g:
-        copy.wait_send()
+
+    @pl.when(inner)
+    def _():
+        for copy in [gone_x[0]] + gone_z + gone_y + passed + [gone_p]:
+            copy.wait_send()
+
+    @pl.when(outer)
+    def _():
+        gone_x[1].wait_send()
+        gone_x[2].wait_send()
 
 
 def on_device(
@@ -556,6 +622,7 @@
             vmem((4, RHS, 128), BF),
             vmem((4, 2, RHS, 128), BF),
             vmem((8, 8, RHS, 128), BF),
+            vmem((RHS, 128), BF),
             vmem((RHS, COLS), F32),
             vmem((32, RHS, 128), F32),
             vmem((32, RHS, 128), BF),
@@ -577,6 +644,8 @@
             dma((3,)),
             dma((7,)),
             dma((7,)),
+            dma,
+            dma,
         ],
         compiler_params=pltpu.CompilerParams(
             collective_id=0, has_side_effects=True, vmem_limit_bytes=60 * 2**20

time: 37.7 us -> 34.4 us (0.912)
  the two profiles are of different devices: /device:TPU:1 before, /device:TPU:24 now
where the time goes in v3:
time: 34.4 us; the launch traced here: 34.3 us
  Pallas kernels  33.5 us (97%)
  local copies, waits for them, and re-layouts  0.8 us (2%)
    pallas_call x1, Pallas kernels, on_device(): pl.pallas_call(kernel, out_shape=pltpu.VMEM((RHS, COLS), BF), in_specs=[a...  33.5 us
    unnamed x1, local copies, waits for them, and re-layouts  0.8 us

profile of v3, /device:TPU:24, one launch (start us, length us, event | category | flops | bytes accessed | tf_op | source)
XLA Modules:
  0.0 34.3 jit_solution(1984442323290726151)
XLA Ops:
  0.0 33.5 %h2_product.1 = bf16[32,8192]{1,0:T(8,128)(2,1)S(1)} custom-call(bf16[32,8192]{1,0:T(8,128)(2,1)} %charges.1, bf16[32,64,256]{2,1,0:T(8,128)(2,1)} %column_basis.1, bf16[32,64,256]{2,1,0:T(8,128)(2,1)} %row_basis.1, bf16[63,64,64]{2,1,0:T(8,128)(2,1)} %local_up.1, bf16[63,64,64]{2,1,0:T(8,128)(2,1)} %local_down.1, s32[8,63]{1,0:T(8,128)} %bitcast.3, ...), custom_call_target="tpu_custom_call" | custom-call | tf_op jit(solution)/shard_map/h2_product/pallas_call | solution.py:603
  33.5 0.8 %copy.15 = bf16[32,8192]{1,0:T(8,128)(2,1)} copy(bf16[32,8192]{1,0:T(8,128)(2,1)S(1)} %h2_product.1) | data formatting | bytes 1048576

commit v4 on v3

--- a/solution.py
+++ b/solution.py
@@ -18,7 +18,7 @@
 COLS = LEAVES * LEAF
 XPARTS = ((0, 1024), (1024, 1024), (2048, 2048), (4096, 2048), (6144, 2048))
 XFIRST = 2
-OWN, REACH, TURN, FAR, REST, FINISH = 4, 16, 96, 16, 8, 16
+OWN, REACH, TURN, FAR, REST, FINISH = 4, 16, 96, 16, 16, 16
 
 
 def nt(a, b):
@@ -238,6 +238,11 @@
 
         batched(4, 4, leaf_moments, keep_moments)
 
+    @pl.when(inner)
+    def _():
+        pl.semaphore_wait(barrier, 12)
+        start(sent[:1])
+
     get_up.wait()
     zero = jnp.zeros((RHS, RANK), F32)
     for height in range(1, LEVELS + 1):
@@ -266,10 +271,6 @@
 
     lifted = nn(root.astype(BF), upv[62])
     rx[x] = jnp.where(low == (x < 2), jnp.concatenate([lifted, lifted], axis=1), 0.0).astype(BF)
-
-    @pl.when(inner)
-    def _():
-        pl.semaphore_wait(barrier, 12)
 
     gone_x = [remote(rx.at[x], rx.at[x], rxsend.at[0], rxrecv.at[0], other)] + [
         remote(rx.at[x], rx.at[x], rxsend.at[1 + k], rxrecv.at[1 + x // 3], p) for k, p in enumerate(middle)
@@ -294,7 +295,7 @@
         for k in range(2)
     ]
     start(moved)
-    pl.when(inner)(lambda: start(sent[:XFIRST]))
+    pl.when(inner)(lambda: start(sent[1:XFIRST]))
     start(sent[XFIRST:])
 
     get_at[0].wait()
@@ -477,33 +478,6 @@
             acc[:, lanes(512 * i + 256 * k, 256)] = got[k]
 
     batched(16, 8, local, keep_rest)
-
-    get_at[2].wait()
-    for copies, (start, size) in zip(sent, XPARTS):
-        arrive(copies)
-
-        def window(i):
-            part = lanes(start + LEAF * i, LEAF)
-            return xin[0, :, part], xin[1, :, part]
-
-        def keep_window(i, got):
-            xw[start // LEAF + i] = got[0]
-            xw[2 * LEAVES + start // LEAF + i] = got[1]
-
-        batched(size // LEAF, 4, window, keep_window)
-
-    def rest(i):
-        totals = []
-        for k in range(2):
-            leaf = 2 * i + k
-            total = acc[:, lanes(256 * leaf, 256)]
-            for n in (1, 2):
-                q = (near_at[n, leaf] - (d - 1) * LEAVES) & 127
-                total = total + nt(xw[q], nbv[leaf, n])
-            totals.append(total)
-        return totals
-
-    batched(16, REST, rest, keep_rest)
 
     get_at[1].wait()
     for copy in get_uc:
@@ -557,14 +531,37 @@
     pl.when(outer)(gone_p.wait_recv)
     parent = pv[...][:, :64]
 
-    def finish(i):
-        part = lanes(512 * i, 512)
-        return (acc[:, part] + nn(parent, qv[:, part])).astype(BF)
-
-    def keep_finish(i, got):
-        out[:, lanes(512 * i, 512)] = got
-
-    batched(16, FINISH, finish, keep_finish)
+    get_at[2].wait()
+    for copies, (start, size) in zip(sent, XPARTS):
+        arrive(copies)
+
+        def window(i):
+            part = lanes(start + LEAF * i, LEAF)
+            return xin[0, :, part], xin[1, :, part]
+
+        def keep_window(i, got):
+            xw[start // LEAF + i] = got[0]
+            xw[2 * LEAVES + start // LEAF + i] = got[1]
+
+        batched(size // LEAF, 4, window, keep_window)
+
+    def rest(i):
+        totals = []
+        above = nn(parent, qv[:, lanes(512 * i, 512)])
+        for k in range(2):
+            leaf = 2 * i + k
+            total = acc[:, lanes(256 * leaf, 256)] + above[:, 256 * k : 256 * (k + 1)]
+            for n in (1, 2):
+                q = (near_at[n, leaf] - (d - 1) * LEAVES) & 127
+                total = total + nt(xw[q], nbv[leaf, n])
+            totals.append(total.astype(BF))
+        return totals
+
+    def keep_out(i, got):
+        for k in range(2):
+            out[:, lanes(512 * i + 256 * k, 256)] = got[k]
+
+    batched(16, REST, rest, keep_out)
 
     for copies in sent:
         leave(copies)

time: 34.4 us -> 30.5 us (0.89)
  the two profiles are of different devices: /device:TPU:24 before, /device:TPU:1 now
where the time goes in v4:
time: 30.5 us; the launch traced here: 30.4 us
  Pallas kernels  29.6 us (97%)
  local copies, waits for them, and re-layouts  0.8 us (3%)
    pallas_call x1, Pallas kernels, on_device(): pl.pallas_call(kernel, out_shape=pltpu.VMEM((RHS, COLS), BF), in_specs=[a...  29.6 us
    unnamed x1, local copies, waits for them, and re-layouts  0.8 us

profile of v4, /device:TPU:1, one launch (start us, length us, event | category | flops | bytes accessed | tf_op | source)
XLA Modules:
  0.0 30.4 jit_solution(11996819223801054465)
XLA Ops:
  0.0 29.6 %h2_product.1 = bf16[32,8192]{1,0:T(8,128)(2,1)S(1)} custom-call(bf16[32,8192]{1,0:T(8,128)(2,1)} %charges.1, bf16[32,64,256]{2,1,0:T(8,128)(2,1)} %column_basis.1, bf16[32,64,256]{2,1,0:T(8,128)(2,1)} %row_basis.1, bf16[63,64,64]{2,1,0:T(8,128)(2,1)} %local_up.1, bf16[63,64,64]{2,1,0:T(8,128)(2,1)} %local_down.1, s32[8,63]{1,0:T(8,128)} %bitcast.3, ...), custom_call_target="tpu_custom_call" | custom-call | tf_op jit(solution)/shard_map/h2_product/pallas_call | solution.py:600
  29.6 0.8 %copy.15 = bf16[32,8192]{1,0:T(8,128)(2,1)} copy(bf16[32,8192]{1,0:T(8,128)(2,1)S(1)} %h2_product.1) | data formatting | bytes 1048576

commit v5 on v4

--- a/solution.py
+++ b/solution.py
@@ -16,7 +16,7 @@
 RANK = 64
 LEVELS = 5
 COLS = LEAVES * LEAF
-XPARTS = ((0, 1024), (1024, 1024), (2048, 2048), (4096, 2048), (6144, 2048))
+XPARTS = ((0, 1024), (1024, 1024), (2048, 2048), (4096, 3072), (7168, 1024))
 XFIRST = 2
 OWN, REACH, TURN, FAR, REST, FINISH = 4, 16, 96, 16, 16, 16
 
@@ -111,6 +111,10 @@
     rgrecv,
     psend,
     precv,
+    hello,
+    hop,
+    hsend,
+    hrecv,
 ):
     g = lax.axis_index("grp")
     s = lax.axis_index("sub")
@@ -132,13 +136,19 @@
     by_y = [(((y + k) % 4) * 2 + core, s) for k in range(1, 4)]
     twin = (2 * y + 1 - core, s)
 
+    first0 = (s == 0) & (g > 0)
+    last15 = (s == 15) & (g < 7)
+    relay3 = (s == 3) & (g < 7)
+
     barrier = pltpu.get_barrier_semaphore()
 
     def greet(peer):
         pl.semaphore_signal(barrier, inc=1, device_id=peer, device_id_type=MESH)
 
-    for there, peer in sides:
-        pl.when(there)(functools.partial(greet, peer))
+    pl.when((d < 127) & jnp.logical_not(last15))(functools.partial(greet, sides[0][1]))
+    pl.when(d > 0)(functools.partial(greet, sides[1][1]))
+    pl.when(first0)(functools.partial(greet, (g - 1, s + 3)))
+    pl.when(relay3)(functools.partial(greet, (g, s + 12)))
 
     @pl.when(inner)
     def _():
@@ -166,7 +176,9 @@
 
     @pl.when(outer)
     def _():
-        pl.semaphore_wait(barrier, 2 + (d < 127).astype(jnp.int32) + (d > 0).astype(jnp.int32))
+        count = 2 + (d < 127).astype(jnp.int32) + ((d > 0) & (s > 0)).astype(jnp.int32)
+        pl.semaphore_wait(barrier, count + (last15 | relay3).astype(jnp.int32))
+        pl.when(last15)(lambda: pl.semaphore_signal(hello, inc=1, device_id=sides[0][1], device_id_type=MESH))
 
     def remote(src, dst, ssem, rsem, peer):
         return pltpu.make_async_remote_copy(
@@ -181,13 +193,19 @@
     def beside(src, dst, ssem, rsem):
         return [remote(src, dst(2 * k), ssem.at[k], rsem.at[k], peer) for k, (_, peer) in enumerate(sides)]
 
-    def start(batches):
+    def start(batches, late=False):
         for k, (there, _) in enumerate(sides):
-
-            @pl.when(there)
-            def _():
-                for copies in batches:
-                    copies[k].start()
+            if late:
+                go = first0 if k else False
+            else:
+                go = there & jnp.logical_not(first0) if k else there
+
+            if go is not False:
+
+                @pl.when(go)
+                def _():
+                    for copies in batches:
+                        copies[k].start()
 
     def arrive(copies):
         for (there, _), copy in zip((sides[1], sides[0]), copies):
@@ -208,6 +226,10 @@
         )
 
     sent = [charges_part(k) for k in range(len(XPARTS))]
+    part = pl.ds(*XPARTS[-1])
+    to_relay = remote(charges.at[:, part], hop, hsend.at[0], hrecv, (g, z * 4 - 9))
+    from_relay = remote(hop, xin.at[0, :, part], hsend.at[1], xrecv.at[len(XPARTS) - 1, 0], (g + 1, s - 3))
+    pl.when(last15)(to_relay.start)
     pl.when(outer)(lambda: start(sent[:XFIRST]))
 
     get_ud = [
@@ -296,7 +318,17 @@
     ]
     start(moved)
     pl.when(inner)(lambda: start(sent[1:XFIRST]))
-    start(sent[XFIRST:])
+    start(sent[XFIRST:-2])
+    pl.when((d < 127) & jnp.logical_not(relay3))(sent[-2][0].start)
+    pl.when((d < 127) & jnp.logical_not(relay3 | last15))(sent[-1][0].start)
+    for copies in sent[-2:]:
+        pl.when((d > 0) & jnp.logical_not(first0))(copies[1].start)
+
+    @pl.when(first0)
+    def _():
+        pl.semaphore_wait(hello, 1)
+        start(sent[:XFIRST] + moved + sent[XFIRST:], late=True)
+
 
     get_at[0].wait()
     t = lax.broadcasted_iota(jnp.int32, (8, 63), 1)
@@ -399,6 +431,14 @@
         qv[:, lanes(512 * i + 256, 256)] = got[1]
 
     batched(16, REACH, reach, keep_reach)
+
+    @pl.when(relay3)
+    def _():
+        to_relay.wait_recv()
+        from_relay.start()
+        sent[-2][0].start()
+        sent[-1][0].start()
+
     for copy in get_ud:
         copy.wait()
     down1 = udv[0]
@@ -528,9 +568,6 @@
         pv[...] = jnp.concatenate([parent, parent], axis=1)
         gone_p.start()
 
-    pl.when(outer)(gone_p.wait_recv)
-    parent = pv[...][:, :64]
-
     get_at[2].wait()
     for copies, (start, size) in zip(sent, XPARTS):
         arrive(copies)
@@ -545,26 +582,58 @@
 
         batched(size // LEAF, 4, window, keep_window)
 
-    def rest(i):
-        totals = []
-        above = nn(parent, qv[:, lanes(512 * i, 512)])
-        for k in range(2):
-            leaf = 2 * i + k
-            total = acc[:, lanes(256 * leaf, 256)] + above[:, 256 * k : 256 * (k + 1)]
-            for n in (1, 2):
-                q = (near_at[n, leaf] - (d - 1) * LEAVES) & 127
-                total = total + nt(xw[q], nbv[leaf, n])
-            totals.append(total.astype(BF))
-        return totals
-
-    def keep_out(i, got):
-        for k in range(2):
-            out[:, lanes(512 * i + 256 * k, 256)] = got[k]
-
-    batched(16, REST, rest, keep_out)
-
-    for copies in sent:
+    def add_near(i, k, total):
+        leaf = 2 * i + k
+        for n in (1, 2):
+            q = (near_at[n, leaf] - (d - 1) * LEAVES) & 127
+            total = total + nt(xw[q], nbv[leaf, n])
+        return total
+
+    upper_first = inner
+
+    @pl.when(upper_first)
+    def _():
+        parent = pv[...][:, :64]
+
+        def rest(i):
+            above = nn(parent, qv[:, lanes(512 * i, 512)])
+            return [
+                add_near(
+                    i, k, acc[:, lanes(512 * i + 256 * k, 256)] + above[:, 256 * k : 256 * (k + 1)]
+                ).astype(BF)
+                for k in range(2)
+            ]
+
+        def keep_out(i, got):
+            for k in range(2):
+                out[:, lanes(512 * i + 256 * k, 256)] = got[k]
+
+        batched(16, REST, rest, keep_out)
+
+    @pl.when(jnp.logical_not(upper_first))
+    def _():
+        def rest(i):
+            return [add_near(i, k, acc[:, lanes(512 * i + 256 * k, 256)]) for k in range(2)]
+
+        batched(16, REST, rest, keep_rest)
+        gone_p.wait_recv()
+        parent = pv[...][:, :64]
+
+        def finish(i):
+            part = lanes(512 * i, 512)
+            return (acc[:, part] + nn(parent, qv[:, part])).astype(BF)
+
+        def keep_finish(i, got):
+            out[:, lanes(512 * i, 512)] = got
+
+        batched(16, FINISH, finish, keep_finish)
+
+    for copies in sent[:-1]:
         leave(copies)
+    pl.when((d < 127) & jnp.logical_not(last15))(sent[-1][0].wait_send)
+    pl.when(d > 0)(sent[-1][1].wait_send)
+    pl.when(last15)(to_relay.wait_send)
+    pl.when(relay3)(from_relay.wait_send)
     for copies in moved:
         leave(copies)
 
@@ -643,6 +712,10 @@
             dma((7,)),
             dma,
             dma,
+            pltpu.SemaphoreType.REGULAR,
+            vmem((RHS, XPARTS[-1][1]), BF),
+            dma((2,)),
+            dma,
         ],
         compiler_params=pltpu.CompilerParams(
             collective_id=0, has_side_effects=True, vmem_limit_bytes=60 * 2**20

time: 30.5 us -> 30 us (0.984)
  the two profiles are of different devices: /device:TPU:1 before, /device:TPU:119 now
where the time goes in v5:
time: 30 us; the launch traced here: 29.9 us
  Pallas kernels  29.1 us (97%)
  local copies, waits for them, and re-layouts  0.8 us (3%)
    pallas_call x1, Pallas kernels, on_device(): pl.pallas_call(kernel, out_shape=pltpu.VMEM((RHS, COLS), BF), in_specs=[a...  29.1 us
    unnamed x1, local copies, waits for them, and re-layouts  0.8 us

profile of v5, /device:TPU:119, one launch (start us, length us, event | category | flops | bytes accessed | tf_op | source)
XLA Modules:
  0.0 29.9 jit_solution(15302037268857698605)
XLA Ops:
  0.0 29.1 %h2_product.1 = bf16[32,8192]{1,0:T(8,128)(2,1)S(1)} custom-call(bf16[32,8192]{1,0:T(8,128)(2,1)} %charges.1, bf16[32,64,256]{2,1,0:T(8,128)(2,1)} %column_basis.1, bf16[32,64,256]{2,1,0:T(8,128)(2,1)} %row_basis.1, bf16[63,64,64]{2,1,0:T(8,128)(2,1)} %local_up.1, bf16[63,64,64]{2,1,0:T(8,128)(2,1)} %local_down.1, s32[8,63]{1,0:T(8,128)} %bitcast.3, ...), custom_call_target="tpu_custom_call" | custom-call | tf_op jit(solution)/shard_map/h2_product/pallas_call | solution.py:669
  29.1 0.8 %copy.15 = bf16[32,8192]{1,0:T(8,128)(2,1)} copy(bf16[32,8192]{1,0:T(8,128)(2,1)S(1)} %h2_product.1) | data formatting | bytes 1048576

commit v6 on v5

--- a/solution.py
+++ b/solution.py
@@ -139,21 +139,24 @@
     first0 = (s == 0) & (g > 0)
     last15 = (s == 15) & (g < 7)
     relay3 = (s == 3) & (g < 7)
+    before15 = (z == 3) & (g < 7) & inner
+    later = first0 | last15
 
     barrier = pltpu.get_barrier_semaphore()
 
     def greet(peer):
         pl.semaphore_signal(barrier, inc=1, device_id=peer, device_id_type=MESH)
 
-    pl.when((d < 127) & jnp.logical_not(last15))(functools.partial(greet, sides[0][1]))
+    pl.when((d < 127) & jnp.logical_not(last15 | before15 & (x == 2)))(functools.partial(greet, sides[0][1]))
     pl.when(d > 0)(functools.partial(greet, sides[1][1]))
     pl.when(first0)(functools.partial(greet, (g - 1, s + 3)))
     pl.when(relay3)(functools.partial(greet, (g, s + 12)))
 
     @pl.when(inner)
     def _():
-        for peer in [other, (g, z * 4), (g, z * 4 + 3)] + by_z + by_y + [twin]:
+        for peer in [other, (g, z * 4)] + by_z + by_y + [twin]:
             greet(peer)
+        pl.when(jnp.logical_not(before15))(functools.partial(greet, (g, z * 4 + 3)))
 
     @pl.when(outer)
     def _():
@@ -177,7 +180,7 @@
     @pl.when(outer)
     def _():
         count = 2 + (d < 127).astype(jnp.int32) + ((d > 0) & (s > 0)).astype(jnp.int32)
-        pl.semaphore_wait(barrier, count + (last15 | relay3).astype(jnp.int32))
+        pl.semaphore_wait(barrier, jnp.where(last15, 2, count + relay3.astype(jnp.int32)))
         pl.when(last15)(lambda: pl.semaphore_signal(hello, inc=1, device_id=sides[0][1], device_id_type=MESH))
 
     def remote(src, dst, ssem, rsem, peer):
@@ -196,9 +199,9 @@
     def start(batches, late=False):
         for k, (there, _) in enumerate(sides):
             if late:
-                go = first0 if k else False
+                go = later if k else False
             else:
-                go = there & jnp.logical_not(first0) if k else there
+                go = there & jnp.logical_not(later) if k else there
 
             if go is not False:
 
@@ -263,6 +266,7 @@
     @pl.when(inner)
     def _():
         pl.semaphore_wait(barrier, 12)
+        pl.when(before15)(lambda: pl.semaphore_signal(hello, inc=1, device_id=(g, 15), device_id_type=MESH))
         start(sent[:1])
 
     get_up.wait()
@@ -304,6 +308,7 @@
 
     @pl.when(outer)
     def _():
+        pl.when(last15)(lambda: pl.semaphore_wait(hello, 2))
         gone_x[1].start()
         gone_x[2].start()
 
@@ -322,12 +327,10 @@
     pl.when((d < 127) & jnp.logical_not(relay3))(sent[-2][0].start)
     pl.when((d < 127) & jnp.logical_not(relay3 | last15))(sent[-1][0].start)
     for copies in sent[-2:]:
-        pl.when((d > 0) & jnp.logical_not(first0))(copies[1].start)
-
-    @pl.when(first0)
-    def _():
-        pl.semaphore_wait(hello, 1)
-        start(sent[:XFIRST] + moved + sent[XFIRST:], late=True)
+        pl.when((d > 0) & jnp.logical_not(later))(copies[1].start)
+
+    pl.when(first0)(lambda: pl.semaphore_wait(hello, 1))
+    start(sent[:XFIRST] + moved + sent[XFIRST:], late=True)
 
 
     get_at[0].wait()

time: 30 us -> 29.2 us (0.973)
  the two profiles are of different devices: /device:TPU:119 before, /device:TPU:1 now
where the time goes in v6:
time: 29.2 us; the launch traced here: 29.1 us
  Pallas kernels  28.2 us (97%)
  local copies, waits for them, and re-layouts  0.8 us (3%)
    pallas_call x1, Pallas kernels, on_device(): pl.pallas_call(kernel, out_shape=pltpu.VMEM((RHS, COLS), BF), in_specs=[a...  28.2 us
    unnamed x1, local copies, waits for them, and re-layouts  0.8 us

profile of v6, /device:TPU:1, one launch (start us, length us, event | category | flops | bytes accessed | tf_op | source)
XLA Modules:
  0.0 29.1 jit_solution(9539678946446391547)
XLA Ops:
  0.0 28.2 %h2_product.1 = bf16[32,8192]{1,0:T(8,128)(2,1)S(1)} custom-call(bf16[32,8192]{1,0:T(8,128)(2,1)} %charges.1, bf16[32,64,256]{2,1,0:T(8,128)(2,1)} %column_basis.1, bf16[32,64,256]{2,1,0:T(8,128)(2,1)} %row_basis.1, bf16[63,64,64]{2,1,0:T(8,128)(2,1)} %local_up.1, bf16[63,64,64]{2,1,0:T(8,128)(2,1)} %local_down.1, s32[8,63]{1,0:T(8,128)} %bitcast.3, ...), custom_call_target="tpu_custom_call" | custom-call | tf_op jit(solution)/shard_map/h2_product/pallas_call | solution.py:672
  28.3 0.8 %copy.15 = bf16[32,8192]{1,0:T(8,128)(2,1)} copy(bf16[32,8192]{1,0:T(8,128)(2,1)S(1)} %h2_product.1) | data formatting | bytes 1048576

commit v7 on v6

--- a/solution.py
+++ b/solution.py
@@ -16,7 +16,7 @@
 RANK = 64
 LEVELS = 5
 COLS = LEAVES * LEAF
-XPARTS = ((0, 1024), (1024, 1024), (2048, 2048), (4096, 3072), (7168, 1024))
+XPARTS = ((0, 1024), (1024, 1024), (2048, 2048), (4096, 2560), (6656, 1536))
 XFIRST = 2
 OWN, REACH, TURN, FAR, REST, FINISH = 4, 16, 96, 16, 16, 16
 
@@ -583,7 +583,7 @@
             xw[start // LEAF + i] = got[0]
             xw[2 * LEAVES + start // LEAF + i] = got[1]
 
-        batched(size // LEAF, 4, window, keep_window)
+        batched(size // LEAF, 2, window, keep_window)
 
     def add_near(i, k, total):
         leaf = 2 * i + k
@@ -592,7 +592,8 @@
             total = total + nt(xw[q], nbv[leaf, n])
         return total
 
-    upper_first = inner
+    upper_first = inner | last15
+    pl.when(last15)(gone_p.wait_recv)
 
     @pl.when(upper_first)
     def _():

time: 29.2 us -> 29 us (level); the launches traced: 29.1 us -> 28.5 us
  Pallas kernels: 28.2 us -> 27.7 us
    pallas_call x1, Pallas kernels: 28.2 us -> 27.7 us  [on_device(): pl.pallas_call(kernel, out_shape=pltpu.VMEM((RHS, COLS), BF), in_specs=[a...]
where the time goes in v7:
time: 29 us; the launch traced here: 28.5 us
  Pallas kernels  27.7 us (96%)
  local copies, waits for them, and re-layouts  0.8 us (3%)
    pallas_call x1, Pallas kernels, on_device(): pl.pallas_call(kernel, out_shape=pltpu.VMEM((RHS, COLS), BF), in_specs=[a...  27.7 us
    unnamed x1, local copies, waits for them, and re-layouts  0.8 us

profile of v7, /device:TPU:1, one launch (start us, length us, event | category | flops | bytes accessed | tf_op | source)
XLA Modules:
  0.0 28.5 jit_solution(8417915750622078343)
XLA Ops:
  0.0 27.7 %h2_product.1 = bf16[32,8192]{1,0:T(8,128)(2,1)S(1)} custom-call(bf16[32,8192]{1,0:T(8,128)(2,1)} %charges.1, bf16[32,64,256]{2,1,0:T(8,128)(2,1)} %column_basis.1, bf16[32,64,256]{2,1,0:T(8,128)(2,1)} %row_basis.1, bf16[63,64,64]{2,1,0:T(8,128)(2,1)} %local_up.1, bf16[63,64,64]{2,1,0:T(8,128)(2,1)} %local_down.1, s32[8,63]{1,0:T(8,128)} %bitcast.3, ...), custom_call_target="tpu_custom_call" | custom-call | tf_op jit(solution)/shard_map/h2_product/pallas_call | solution.py:673
  27.7 0.8 %copy.15 = bf16[32,8192]{1,0:T(8,128)(2,1)} copy(bf16[32,8192]{1,0:T(8,128)(2,1)S(1)} %h2_product.1) | data formatting | bytes 1048576

commit v8 on v7

--- a/solution.py
+++ b/solution.py
@@ -149,8 +149,8 @@
 
     pl.when((d < 127) & jnp.logical_not(last15 | before15 & (x == 2)))(functools.partial(greet, sides[0][1]))
     pl.when(d > 0)(functools.partial(greet, sides[1][1]))
-    pl.when(first0)(functools.partial(greet, (g - 1, s + 3)))
-    pl.when(relay3)(functools.partial(greet, (g, s + 12)))
+    pl.when(first0)(functools.partial(greet, ((g + 7) % 8, 3)))
+    pl.when(relay3)(functools.partial(greet, (g, 15)))
 
     @pl.when(inner)
     def _():
@@ -230,8 +230,8 @@
 
     sent = [charges_part(k) for k in range(len(XPARTS))]
     part = pl.ds(*XPARTS[-1])
-    to_relay = remote(charges.at[:, part], hop, hsend.at[0], hrecv, (g, z * 4 - 9))
-    from_relay = remote(hop, xin.at[0, :, part], hsend.at[1], xrecv.at[len(XPARTS) - 1, 0], (g + 1, s - 3))
+    to_relay = remote(charges.at[:, part], hop, hsend.at[0], hrecv, (g, 3))
+    from_relay = remote(hop, xin.at[0, :, part], hsend.at[1], xrecv.at[len(XPARTS) - 1, 0], ((g + 1) % 8, 0))
     pl.when(last15)(to_relay.start)
     pl.when(outer)(lambda: start(sent[:XFIRST]))
 

time: 29 us -> 29 us (level)
  no operation moved by 1% of the time
where the time goes in v8:
time: 29 us; the launch traced here: 28.5 us
  Pallas kernels  27.7 us (96%)
  local copies, waits for them, and re-layouts  0.8 us (3%)
    pallas_call x1, Pallas kernels, on_device(): pl.pallas_call(kernel, out_shape=pltpu.VMEM((RHS, COLS), BF), in_specs=[a...  27.7 us
    unnamed x1, local copies, waits for them, and re-layouts  0.8 us

profile of v8, /device:TPU:1, one launch (start us, length us, event | category | flops | bytes accessed | tf_op | source)
XLA Modules:
  0.0 28.5 jit_solution(14017488007218249032)
XLA Ops:
  0.0 27.7 %h2_product.1 = bf16[32,8192]{1,0:T(8,128)(2,1)S(1)} custom-call(bf16[32,8192]{1,0:T(8,128)(2,1)} %charges.1, bf16[32,64,256]{2,1,0:T(8,128)(2,1)} %column_basis.1, bf16[32,64,256]{2,1,0:T(8,128)(2,1)} %row_basis.1, bf16[63,64,64]{2,1,0:T(8,128)(2,1)} %local_up.1, bf16[63,64,64]{2,1,0:T(8,128)(2,1)} %local_down.1, s32[8,63]{1,0:T(8,128)} %bitcast.3, ...), custom_call_target="tpu_custom_call" | custom-call | tf_op jit(solution)/shard_map/h2_product/pallas_call | solution.py:673
  27.7 0.8 %copy.15 = bf16[32,8192]{1,0:T(8,128)(2,1)} copy(bf16[32,8192]{1,0:T(8,128)(2,1)S(1)} %h2_product.1) | data formatting | bytes 1048576

commit v9 on v8

--- a/solution.py
+++ b/solution.py
@@ -172,7 +172,7 @@
         return copy
 
     get_x = [load(charges.at[:, pl.ds(4096 * k, 4096)], cx.at[:, pl.ds(4096 * k, 4096)]) for k in range(2)]
-    get_cb = [load(column_basis.at[pl.ds(8 * k, 8)], cbv.at[pl.ds(8 * k, 8)]) for k in range(4)]
+    get_cb = [load(column_basis.at[pl.ds(16 * k, 16)], cbv.at[pl.ds(16 * k, 16)]) for k in range(2)]
     get_up = load(local_up, upv)
     get_uu = load(upper_up, uuv)
     get_at = [load(local_far, far_raw), load(upper_far, ufar_at), load(near_source, near_at)]
@@ -244,24 +244,23 @@
 
     low = lax.broadcasted_iota(jnp.int32, (RHS, 128), 1) < 64
 
-    for k in range(4):
-        if k % 2 == 0:
-            get_x[k // 2].wait()
+    for k in range(2):
+        get_x[k].wait()
         get_cb[k].wait()
 
         def leaf_moments(i):
-            at = 4 * k + i
+            at = 8 * k + i
             one, two = cx[:, lanes(512 * at, 256)], cx[:, lanes(512 * at + 256, 256)]
             both = nt(jnp.concatenate([one, two], axis=0), cbv[pl.ds(2 * at, 2)].reshape(128, LEAF))
             return one, two, jnp.where(low, both[:RHS], both[RHS:]).astype(BF)
 
         def keep_moments(i, got):
-            at = 4 * k + i
+            at = 8 * k + i
             xw[LEAVES + 2 * at] = got[0]
             xw[LEAVES + 2 * at + 1] = got[1]
             mv[32 + at] = got[2]
 
-        batched(4, 4, leaf_moments, keep_moments)
+        batched(8, 8, leaf_moments, keep_moments)
 
     @pl.when(inner)
     def _():

time: 29 us -> 29 us (level)
  no operation moved by 1% of the time
where the time goes in v9:
time: 29 us; the launch traced here: 28.5 us
  Pallas kernels  27.7 us (96%)
  local copies, waits for them, and re-layouts  0.8 us (3%)
    pallas_call x1, Pallas kernels, on_device(): pl.pallas_call(kernel, out_shape=pltpu.VMEM((RHS, COLS), BF), in_specs=[a...  27.7 us
    unnamed x1, local copies, waits for them, and re-layouts  0.8 us

profile of v9, /device:TPU:1, one launch (start us, length us, event | category | flops | bytes accessed | tf_op | source)
XLA Modules:
  0.0 28.5 jit_solution(6480566750964620549)
XLA Ops:
  0.0 27.7 %h2_product.1 = bf16[32,8192]{1,0:T(8,128)(2,1)S(1)} custom-call(bf16[32,8192]{1,0:T(8,128)(2,1)} %charges.1, bf16[32,64,256]{2,1,0:T(8,128)(2,1)} %column_basis.1, bf16[32,64,256]{2,1,0:T(8,128)(2,1)} %row_basis.1, bf16[63,64,64]{2,1,0:T(8,128)(2,1)} %local_up.1, bf16[63,64,64]{2,1,0:T(8,128)(2,1)} %local_down.1, s32[8,63]{1,0:T(8,128)} %bitcast.3, ...), custom_call_target="tpu_custom_call" | custom-call | tf_op jit(solution)/shard_map/h2_product/pallas_call | solution.py:672
  27.7 0.8 %copy.15 = bf16[32,8192]{1,0:T(8,128)(2,1)} copy(bf16[32,8192]{1,0:T(8,128)(2,1)S(1)} %h2_product.1) | data formatting | bytes 1048576
